TPU v7x, 512 devices: a whole 4x4x16 slice. The times are simulated.
512 devices in a mesh: mer: 64 (over y, z), grp: 2 (over x_hi), box: 4 (over x_lo, core).
Axes of the slice: x: 4 (x_hi: 2, x_lo: 2; x = x_hi * 2 + x_lo), y: 4, z: 16, core: 2. Of those that a mesh axis runs over, the one named last changes fastest.
Arguments:
- displacement: float32 [1024, 5, 5, 1024], P(('mer', 'grp', 'box')), may hold values from -0.2 to 0.2
- radius: float32 [1024, 5, 5], P(('mer', 'grp', 'box')), may hold values from 128 to 1024
- bulk_modulus: bfloat16 [1024, 5, 5, 1024], P(('mer', 'grp', 'box')), may hold values from 0.5 to 2
- inverse_mass: float32 [1024, 5, 5], P(('mer', 'grp', 'box')), may hold values from 0.5 to 2
- order_counts: int32 [1024], P(('mer', 'grp', 'box')), may hold values from 128 to 512
- source_point: int32 [65536], P(('mer', 'grp', 'box')), may hold values from 0 to 49
- route_owner: int32 [65536, 1], P(('mer', 'grp', 'box')), may hold values from 0 to 63; in each aligned block of 128 rows (0 to 127, 128 to 255, ...) at most 8 rows name the same one
- face_slot: int32 [65536], P(('mer', 'grp', 'box')), may hold values from 0 to 15
- window_start: int32 [65536], P(('mer', 'grp', 'box')), may hold values from 0 to 992
- box_field: float32 [2048, 64, 256], P('mer', 'box', 'grp'), may hold values from -6 to 6
- box_speed: float32 [2048, 64, 256], P('mer', 'box', 'grp'), may hold values from 0.25 to 1
Outputs:
- global_accel: float32 [1024, 5, 5, 1024], P(('mer', 'grp', 'box'))
- box_accel: float32 [2048, 64, 256], P('mer', 'box', 'grp')
Inputs may be any that keep to these rules, and one draw needn't show every extreme that they name: `route_owner`: among the 128 records of one device no owner is named more than 8 times, a bound that some block reaches.
All inputs are finite; a program needn't handle non-finite values.
Results may differ from a plain program's by a relative error of at most 0.004.
Values may be sent and summed in bfloat16 or wider, within the bound.
A program may use at most 64 MiB of HBM per device.

v0:
```python
import math

import jax
import jax.numpy as jnp
import numpy as np
from jax import lax
from jax.sharding import PartitionSpec as P

TRACTION_SCALE = 0.25
HIGHEST = lax.Precision.HIGHEST


def shifted(block, axis, distance):
    devices = range(lax.axis_size(axis))
    route = [(i - distance, i) for i in devices if i - distance in devices]
    return lax.ppermute(block, axis, route)


def padded_2(shard, sides, width):
    for axis, dim in sides:
        count, length = (lax.axis_size(axis), shard.shape[dim])
        up = [(i, (i + 1) % count) for i in range(count - 1)]
        down = [(j, i) for i, j in up]
        last = lax.slice_in_dim(shard, length - width, length, axis=dim)
        first = lax.slice_in_dim(shard, 0, width, axis=dim)
        before = lax.ppermute(last, axis, up)
        after = lax.ppermute(first, axis, down)
        shard = jnp.concatenate([before, shard, after], axis=dim)
    return shard


def gll_derivative():
    gll_nodes = np.array([-1.0, -math.sqrt(3.0 / 7.0), 0.0, math.sqrt(3.0 / 7.0), 1.0])
    legendre = (35.0 * gll_nodes**4 - 30.0 * gll_nodes**2 + 3.0) / 8.0
    npoints = gll_nodes.shape[0]
    degree = npoints - 1
    deriv_table = np.zeros((npoints, npoints))
    for row_index in range(npoints):
        for col_index in range(npoints):
            if row_index != col_index:
                deriv_table[row_index, col_index] = legendre[row_index] / (
                    legendre[col_index] * (gll_nodes[row_index] - gll_nodes[col_index])
                )
    deriv_table[0, 0] = -degree * (degree + 1) / 4.0
    deriv_table[-1, -1] = degree * (degree + 1) / 4.0
    return deriv_table.astype(np.float32)


def azimuth_tables(orders_total):
    samples = 2 * orders_total
    order_ids = jnp.arange(orders_total, dtype=jnp.int32)
    sample_ids = jnp.arange(samples, dtype=jnp.int32)
    product = order_ids[:, None] * sample_ids[None, :] % samples
    angles = product.astype(jnp.float32) * (2.0 * math.pi / samples)
    cosine = jnp.cos(angles)
    sine = jnp.sin(angles)
    weights = jnp.where(order_ids == 0, 1.0, 2.0).astype(jnp.float32)[:, None]
    synthesis = jnp.concatenate([weights * cosine, -weights * sine], axis=0).astype(jnp.bfloat16)
    analysis = (jnp.concatenate([cosine, -sine], axis=0).T / samples).astype(jnp.bfloat16)
    return (synthesis, analysis)


def element_force(field, radius, modulus, mask, deriv, synthesis, analysis):
    orders_total = field.shape[-1] // 2
    order_vals = jnp.arange(orders_total).astype(jnp.float32)
    masked = field * mask[:, None, None, :]
    grad_first = jnp.einsum("ac,ecbk->eabk", deriv, masked, precision=HIGHEST)
    grad_second = jnp.einsum("bc,eack->eabk", deriv, masked, precision=HIGHEST)
    inverse_radius = (1.0 / radius)[..., None]
    grad_azimuth = (
        jnp.concatenate(
            [-order_vals * masked[..., orders_total:], order_vals * masked[..., :orders_total]],
            axis=-1,
        )
        * inverse_radius
    )
    gradient = jnp.stack([grad_first, grad_second, grad_azimuth]).astype(jnp.bfloat16)
    grad_shape = gradient.shape
    physical = jnp.dot(
        gradient.reshape(-1, grad_shape[-1]), synthesis, preferred_element_type=jnp.float32
    )
    physical = physical.reshape(grad_shape[:-1] + (synthesis.shape[1],))
    stress = (modulus[None].astype(jnp.float32) * physical).astype(jnp.bfloat16)
    coeffs = jnp.dot(
        stress.reshape(-1, stress.shape[-1]), analysis, preferred_element_type=jnp.float32
    )
    coeffs = coeffs.reshape(grad_shape) * mask[None, :, None, None, :]
    divergence = jnp.einsum("ca,ecbk->eabk", deriv, coeffs[0], precision=HIGHEST)
    divergence = divergence + jnp.einsum("cb,eack->eabk", deriv, coeffs[1], precision=HIGHEST)
    azimuth_part = coeffs[2]
    divergence = (
        divergence
        + jnp.concatenate(
            [
                order_vals * azimuth_part[..., orders_total:],
                -order_vals * azimuth_part[..., :orders_total],
            ],
            axis=-1,
        )
        * inverse_radius
    )
    return (masked, coeffs[1], divergence)


def shards(
    displacement,
    radius,
    bulk_modulus,
    inverse_mass,
    order_counts,
    source_point,
    route_owner,
    face_slot,
    window_start,
    box_field,
    box_speed,
):
    orders_total = displacement.shape[-1] // 2
    samples = 2 * orders_total
    deriv = jnp.asarray(gll_derivative())
    synthesis, analysis = azimuth_tables(orders_total)
    order_ids = jnp.arange(samples, dtype=jnp.int32) % orders_total
    mask = (order_ids[None, :] < order_counts[:, None]).astype(jnp.float32)
    masked, traction, divergence = element_force(
        displacement, radius, bulk_modulus, mask, deriv, synthesis, analysis
    )
    from_below = shifted(divergence[-1, -1], ("mer", "grp", "box"), 1)
    from_above = shifted(divergence[0, 0], ("mer", "grp", "box"), -1)
    below_rows = jnp.concatenate([from_below[None], divergence[:-1, -1]], axis=0)
    above_rows = jnp.concatenate([divergence[1:, 0], from_above[None]], axis=0)
    assembled = divergence.at[:, 0].add(below_rows).at[:, -1].add(above_rows)
    global_accel = -inverse_mass[..., None] * assembled
    n_mer = lax.axis_size("mer")
    records = source_point.shape[0]
    capacity = max(2, 4 * records // n_mer)
    width_x = box_field.shape[0]
    width_y = box_field.shape[1]
    owners = route_owner[:, 0]
    npoints = displacement.shape[0] * displacement.shape[1] * displacement.shape[2]
    flat_field = masked.reshape(npoints, samples)
    flat_trac = traction.reshape(npoints, samples)
    sources = jnp.stack([flat_field[source_point], flat_trac[source_point]], axis=1).astype(
        jnp.bfloat16
    )
    owner_hits = (owners[:, None] == jnp.arange(n_mer, dtype=jnp.int32)[None, :]).astype(jnp.int32)
    earlier = jnp.cumsum(owner_hits, axis=0) - owner_hits
    position = owners * capacity + jnp.sum(earlier * owner_hits, axis=1)
    slot_send = (
        jnp.zeros((n_mer * capacity,), jnp.int32)
        .at[position]
        .set(face_slot)
        .reshape(n_mer, capacity)
    )
    offsets = jnp.arange(width_x, dtype=jnp.int32)
    sample_rows = synthesis.T
    leading = sources.shape[:-2]
    count = sources.shape[0]
    block = math.gcd(count, 64)

    def one_block(pieces):
        part_coeffs, part_starts = pieces
        table = sample_rows[part_starts[:, None] + offsets[None, :]]
        return jnp.einsum(
            "bik,bjk->bij", part_coeffs, table, preferred_element_type=jnp.float32
        ).astype(jnp.bfloat16)

    result = lax.map(
        one_block,
        (
            sources.reshape((count // block, block, 2, samples)),
            window_start.reshape((count // block, block)),
        ),
    )
    local_values = result.reshape(leading + (2, width_x))
    value_send = (
        jnp.zeros((n_mer * capacity, 2, width_x), jnp.bfloat16).at[position].set(local_values)
    )
    value_send = value_send.reshape(n_mer, capacity, 2, width_x)
    values, slot_ids = (
        lax.all_to_all(value_send, "mer", split_axis=0, concat_axis=0, tiled=True),
        lax.all_to_all(slot_send, "mer", split_axis=0, concat_axis=0, tiled=True),
    )
    selection = (
        slot_ids.reshape(-1)[:, None] == jnp.arange(width_y, dtype=jnp.int32)[None, :]
    ).astype(jnp.float32)
    faces = jnp.einsum(
        "ry,rqx->qxy",
        selection,
        values.reshape(-1, 2, width_x).astype(jnp.float32),
        precision=HIGHEST,
    )
    padded = padded_2(
        box_field.astype(jnp.bfloat16), (("mer", 0), ("grp", 2), ("box", 1)), 1
    ).astype(box_field.dtype)
    group_index = lax.axis_index("grp")
    is_low = (group_index == 0).astype(jnp.float32)
    is_high = (group_index == lax.axis_size("grp") - 1).astype(jnp.float32)
    padded = (
        padded.at[1:-1, 1:-1, 0].add(is_low * faces[0]).at[1:-1, 1:-1, -1].add(is_high * faces[0])
    )
    neighbours = padded[2:, 1:-1, 1:-1] + padded[:-2, 1:-1, 1:-1]
    neighbours = neighbours + padded[1:-1, 2:, 1:-1] + padded[1:-1, :-2, 1:-1]
    neighbours = neighbours + padded[1:-1, 1:-1, 2:] + padded[1:-1, 1:-1, :-2]
    box_accel = box_speed * (neighbours - 6.0 * box_field)
    box_accel = box_accel.at[:, :, 0].add(is_low * (TRACTION_SCALE * faces[1]))
    box_accel = box_accel.at[:, :, -1].add(is_high * (TRACTION_SCALE * faces[1]))
    return (global_accel, box_accel)


def solution(mesh):
    return jax.shard_map(
        shards,
        mesh=mesh,
        in_specs=(
            P(("mer", "grp", "box"), None, None, None),
            P(("mer", "grp", "box"), None, None),
            P(("mer", "grp", "box"), None, None, None),
            P(("mer", "grp", "box"), None, None),
            P(("mer", "grp", "box")),
            P(("mer", "grp", "box")),
            P(("mer", "grp", "box"), None),
            P(("mer", "grp", "box")),
            P(("mer", "grp", "box")),
            P("mer", "box", "grp"),
            P("mer", "box", "grp"),
        ),
        out_specs=(P(("mer", "grp", "box"), None, None, None), P("mer", "box", "grp")),
        check_vma=False,
    )
```

profile of v0, /device:TPU:6, one launch (start us, length us, event | category | flops | bytes accessed | tf_op | source)
XLA Modules:
  0.0 167.3 jit_solution(12029645373989953401)
XLA Ops:
  0.6 1.0 convert_element_type.79
  2.2 4.4 %collective-permute-start.2 = (bf16[1,16,128]{2,1,0:T(8,128)(2,1)}, bf16[1,16,128]{2,1,0:T(8,128)(2,1)}, u32[]{:S(2)}, u32[]{:S(2)}) collective-permute-start(bf16[1,16,128]{2,1,0:T(8,128)(2,1)} %get-tuple-element.179), channel_id=1, source_target_pairs={{0,8},{8,16},{16,24},{24,32},{32,40},{40,48},{48,56},{56,64},{64,7... | collective-permute-start | bytes 12296 | tf_op jit(solution)/shard_map/ppermute | solution.py:26
  6.6 1.3 collective-permute-start.3
  7.9 0.7 fusion.52
  8.8 0.8 select_reduce_fusion
  10.3 1.1 scatter_custom_fusion.1
  12.1 20.4 %all-to-all-start.1 = ((s32[64,1,8]{2,1,0:T(1,128)}), s32[64,1,8]{2,1,0:T(1,128)}, u32[]{:S(2)}, u32[]{:S(2)}) async-start(s32[64,1,8]{2,1,0:T(1,128)} %bitcast.36), calls=%async_computation.1 | async-start | bytes 65536 | tf_op jit(solution)/shard_map/all_to_all | solution.py:181
  32.5 0.7 compare_convert_fusion
  33.3 1.0 broadcast_multiply_fusion.1
  34.3 1.2 convolution_convert_fusion.1
  35.4 1.2 convolution_convert_fusion.2
  36.6 9.2 %fusion.31 = (f32[512,1024]{1,0:T(8,128)}, f32[512,1024]{1,0:T(8,128)}) fusion(), kind=kLoop, calls=%fused_computation.49 | loop fusion | flops 7864320 | bytes 4194304 | tf_op jit(solution)/shard_map/cos | solution.py:55
  46.2 0.8 copy.135
  47.1 8.7 %multiply_convert_fusion = (bf16[512,1024]{1,0:T(8,128)(2,1)S(1)}, bf16[512,1024]{1,0:T(8,128)(2,1)S(1)}) fusion(f32[512]{0:T(512)S(1)} %fusion.65, f32[512]{0:T(512)S(1)} %fusion.62), kind=kLoop, calls=%fused_computation.31 | loop fusion | flops 9437184 | bytes 2101248 | tf_op jit(solution)/shard_map/convert.5
  55.9 1.2 pad_maximum_fusion.3
  57.1 4.3 %fusion.13 = f32[3,2,5,5,1024]{4,3,2,1,0:T(8,128)S(1)} fusion(f32[512,1024]{1,0:T(8,128)} %get-tuple-element.184, f32[512,1024]{1,0:T(8,128)} %get-tuple-element.183, bf16[512,1024]{1,0:T(8,128)(2,1)S(1)} %get-tuple-element.181, bf16[512,1024]{1,0:T(8,128)(2,1)S(1)} %get-tuple-element.182, bf16[3,2,5,5,1024]{4,1,3,2,0:T(2,128)(2,1)} %pad_maximum_fusion.3, ...), kind=kOutput, calls=%fused_computation.26 | convolution fusion | flops 636792832 | bytes 7417856 | tf_op jit(solution)/shard_map/dot_general | solution.py:84
  64.2 1.9 %collective-permute-start = (f32[5,1024]{1,0:T(8,128)}, f32[5,1024]{1,0:T(8,128)}, u32[]{:S(2)}, u32[]{:S(2)}) collective-permute-start(f32[5,1024]{1,0:T(8,128)} %bitcast.118), channel_id=1, source_target_pairs={{0,1},{1,2},{2,3},{3,4},{4,5},{5,6},{6,7},{7,8},{8,9},{9,10},{10,1... | collective-permute-start | bytes 61448 | tf_op jit(solution)/shard_map/ppermute | solution.py:16
  66.8 3.9 %collective-permute-start.1 = (f32[5,1024]{1,0:T(8,128)}, f32[5,1024]{1,0:T(8,128)}, u32[]{:S(2)}, u32[]{:S(2)}) collective-permute-start(f32[5,1024]{1,0:T(8,128)} %bitcast.119), channel_id=1, source_target_pairs={{1,0},{2,1},{3,2},{4,3},{5,4},{6,5},{7,6},{8,7},{9,8},{10,9},{11,1... | collective-permute-start | bytes 61448 | tf_op jit(solution)/shard_map/ppermute | solution.py:16
  70.7 1.5 fusion.21
  72.5 0.9 gather_fusion.2
  73.8 0.9 gather_fusion.1
  76.3 1.3 collective-permute-start.4
  77.6 6.0 %collective-permute-start.5 = (bf16[34,16,1]{0,1,2:T(8,128)(2,1)S(1)}, bf16[34,16,1]{0,1,2:T(8,128)(2,1)S(1)}, u32[]{:S(2)}, u32[]{:S(2)}) collective-permute-start(bf16[34,16,1]{0,1,2:T(8,128)(2,1)S(1)} %get-tuple-element.170), channel_id=1, source_target_pairs={{4,0},{5,1},{6,2},{7,3},{12,8},{13,9},{14,10},{15,11},{20,16},{21,... | collective-permute-start | bytes 3272 | tf_op jit(solution)/shard_map/ppermute | solution.py:27
  83.7 1.2 pad_maximum_fusion.2
  84.9 2.9 %copy.162 = bf16[1024,1024]{1,0:T(8,128)(2,1)S(1)} copy(bf16[1024,1024]{0,1:T(8,128)(2,1)} %fusion.21) | data formatting | bytes 4194304
  87.9 0.8 pad_maximum_fusion.7
  88.7 1.9 %collective-permute-start.6 = (bf16[34,1,130]{0,1,2:T(2,128)(2,1)}, bf16[34,1,130]{0,1,2:T(2,128)(2,1)S(1)}, u32[]{:S(2)}, u32[]{:S(2)}) collective-permute-start(bf16[34,1,130]{0,1,2:T(2,128)(2,1)} %get-tuple-element.167), channel_id=1, source_target_pairs={{0,1},{1,2},{2,3},{4,5},{5,6},{6,7},{8,9},{9,10},{10,11},{12,13},{... | collective-permute-start | bytes 26528 | tf_op jit(solution)/shard_map/ppermute | solution.py:26
  90.6 3.6 %collective-permute-start.7 = (bf16[34,1,130]{0,1,2:T(2,128)(2,1)}, bf16[34,1,130]{0,1,2:T(2,128)(2,1)}, u32[]{:S(2)}, u32[]{:S(2)}) collective-permute-start(bf16[34,1,130]{0,1,2:T(2,128)(2,1)} %get-tuple-element.168), channel_id=1, source_target_pairs={{1,0},{2,1},{3,2},{5,4},{6,5},{7,6},{9,8},{10,9},{11,10},{13,12},{... | collective-permute-start | bytes 26528 | tf_op jit(solution)/shard_map/ppermute | solution.py:27
  94.2 27.6 %while.17 = (s32[]{:T(128)}, bf16[2,64,2,32]{3,2,1,0:T(2,128)(2,1)}, bf16[2,64,2,1024]{3,2,1,0:T(2,128)(2,1)S(1)}, s32[2,64]{1,0:T(2,128)S(1)}, bf16[1024,1024]{1,0:T(8,128)(2,1)S(1)}, /*index=5*/s32[]{:T(128)}) while((s32[]{:T(128)}, bf16[2,64,2,32]{3,2,1,0:T(2,128)(2,1)}, bf16[2,64,2,1024]{3,2,1,0:T(2,128)(2,1)S(1)}, ...), condition=%wide.region_3.4_spmd.clone, body=%wide.region_2.3_spmd.clone.sunk | while | flops 8402946 | bytes 12928841 | solution.py:167
  94.4 9.6 %gather_fusion = bf16[2048,1024]{1,0:T(8,128)(2,1)} fusion(bf16[1024,1024]{1,0:T(8,128)(2,1)S(1)} %get-tuple-element.232, s32[2048]{0:T(1024)S(1)} %broadcast_clamp_fusion.2), kind=kCustom, calls=%fused_computation.clone.clone.1 | custom fusion | bytes 8396800 | tf_op jit(solution)/shard_map/while/body/eval_jaxpr/gather | solution.py:162
  104.1 4.0 %fusion.88 = bf16[2,64,2,32]{3,2,1,0:T(2,128)(2,1)} fusion(bf16[2,64,2,32]{3,2,1,0:T(2,128)(2,1)} %get-tuple-element.223, s32[]{:T(128)} %get-tuple-element.222, bf16[64,32,1024]{2,1,0:T(8,128)(2,1)} %bitcast.131, bf16[2,64,2,1024]{3,2,1,0:T(2,128)(2,1)S(1)} %get-tuple-element.230), kind=kOutput, calls=%fused_computation.8.clone.1 | convolution fusion | flops 8392704 | bytes 4490240 | tf_op jit(solution)/shard_map/while/body/eval_jaxpr/bik,bjk->bij/dot_general | solution.py:163
  108.2 9.6 %gather_fusion = bf16[2048,1024]{1,0:T(8,128)(2,1)} fusion(bf16[1024,1024]{1,0:T(8,128)(2,1)S(1)} %get-tuple-element.232, s32[2048]{0:T(1024)S(1)} %broadcast_clamp_fusion.2), kind=kCustom, calls=%fused_computation.clone.clone.1 | custom fusion | bytes 8396800 | tf_op jit(solution)/shard_map/while/body/eval_jaxpr/gather | solution.py:162
  117.9 4.0 %fusion.88 = bf16[2,64,2,32]{3,2,1,0:T(2,128)(2,1)} fusion(bf16[2,64,2,32]{3,2,1,0:T(2,128)(2,1)} %get-tuple-element.223, s32[]{:T(128)} %get-tuple-element.222, bf16[64,32,1024]{2,1,0:T(8,128)(2,1)} %bitcast.131, bf16[2,64,2,1024]{3,2,1,0:T(2,128)(2,1)S(1)} %get-tuple-element.230), kind=kOutput, calls=%fused_computation.8.clone.1 | convolution fusion | flops 8392704 | bytes 4490240 | tf_op jit(solution)/shard_map/while/body/eval_jaxpr/bik,bjk->bij/dot_general | solution.py:163
  121.9 2.4 %copy.168 = f32[32,16,128]{0,1,2:T(8,128)} copy(f32[32,16,128]{2,1,0:T(8,128)} %param.35) | data formatting | bytes 524288 | tf_op args[9]
  124.5 4.4 %scatter_fusion = bf16[512,2,32]{2,1,0:T(2,128)(2,1)S(1)} fusion(bf16[512,2,32]{2,1,0:T(2,128)(2,1)S(1)} %broadcast_in_dim.25, s32[128]{0:T(128)S(1)} %copy-done.7, bf16[128,2,32]{2,1,0:T(2,128)(2,1)S(1)} %bitcast.140), kind=kCustom, calls=%fused_computation.3 | custom fusion | bytes 49664 | tf_op jit(solution)/shard_map/scatter | solution.py:176
  129.0 0.8 reshape.507
  129.8 1.4 copy.169
  131.3 15.3 %all-to-all-start = ((bf16[64,2,256]{2,1,0:T(2,128)(2,1)}), bf16[64,2,256]{2,1,0:T(2,128)(2,1)S(1)}, u32[]{:S(2)}, u32[]{:S(2)}) async-start(bf16[64,2,256]{2,1,0:T(2,128)(2,1)} %reshape.507), calls=%async_computation | async-start | bytes 131072 | tf_op jit(solution)/shard_map/all_to_all | solution.py:180
  147.2 1.5 reduce.15
  148.8 1.3 maximum_convert_fusion
  150.1 0.8 fusion.51
  150.9 0.8 fusion.50
  151.8 0.8 copy.170
  152.6 8.5 %all-to-all-done = bf16[64,2,256]{2,1,0:T(2,128)(2,1)S(1)} async-done(((bf16[64,2,256]{2,1,0:T(2,128)(2,1)}), bf16[64,2,256]{2,1,0:T(2,128)(2,1)S(1)}, u32[]{:S(2)}, u32[]{:S(2)}) %all-to-all-start) | async-done | bytes 65568 | tf_op jit(solution)/shard_map/all_to_all | solution.py:180
  161.5 0.7 scatter-add.24
  162.4 0.7 scatter-add.25
  163.1 3.0 %fusion.29 = f32[32,16,128]{0,1,2:T(8,128)S(1)} fusion(f32[32,16,128]{0,1,2:T(8,128)} %copy.169, f32[34,18,130]{0,1,2:T(8,128)S(1)} %scatter-add.25, f32[32,16,128]{0,1,2:T(8,128)} %copy.168), kind=kLoop, calls=%fused_computation.43 | loop fusion | flops 524288 | bytes 2359296 | tf_op jit(solution)/shard_map/mul | solution.py:204
  166.1 1.2 copy.171
  (90 shorter events, 10.3 us)
Async XLA Ops:
  2.2 72.9 %collective-permute-start.2 = (bf16[1,16,128]{2,1,0:T(8,128)(2,1)}, bf16[1,16,128]{2,1,0:T(8,128)(2,1)}, u32[]{:S(2)}, u32[]{:S(2)}) collective-permute-start(bf16[1,16,128]{2,1,0:T(8,128)(2,1)} %get-tuple-element.179), channel_id=1, source_target_pairs={{0,8},{8,16},{16,24},{24,32},{32,40},{40,48},{48,56},{56,64},{64,7... | collective-permute-start | bytes 12296 | tf_op jit(solution)/shard_map/ppermute | solution.py:26
  6.6 68.5 %collective-permute-start.3 = (bf16[1,16,128]{2,1,0:T(8,128)(2,1)}, bf16[1,16,128]{2,1,0:T(8,128)(2,1)}, u32[]{:S(2)}, u32[]{:S(2)}) collective-permute-start(bf16[1,16,128]{2,1,0:T(8,128)(2,1)} %get-tuple-element.180), channel_id=1, source_target_pairs={{8,0},{16,8},{24,16},{32,24},{40,32},{48,40},{56,48},{64,56},{72,6... | collective-permute-start | bytes 12296 | tf_op jit(solution)/shard_map/ppermute | solution.py:27
  10.3 22.2 %copy-start.6 = (s32[128]{0:T(128)}, s32[128]{0:T(128)S(1)}, u32[]{:S(2)}) copy-start(s32[128]{0:T(128)S(1)} %fusion.67) | copy-start | bytes 1540
  12.1 119.2 %all-to-all-start.1 = ((s32[64,1,8]{2,1,0:T(1,128)}), s32[64,1,8]{2,1,0:T(1,128)}, u32[]{:S(2)}, u32[]{:S(2)}) async-start(s32[64,1,8]{2,1,0:T(1,128)} %bitcast.36), calls=%async_computation.1 | async-start | bytes 65536 | tf_op jit(solution)/shard_map/all_to_all | solution.py:181
  36.6 9.2 %copy-start.4 = (f32[2,5,5]{2,0,1:T(2,128)S(1)}, f32[2,5,5]{2,0,1:T(2,128)}, u32[]{:S(2)}) copy-start(f32[2,5,5]{2,0,1:T(2,128)} %param.27) | copy-start | bytes 604
  36.6 9.6 %copy-start.1 = (bf16[2,5,5,1024]{3,0,2,1:T(2,128)(2,1)S(1)}, bf16[2,5,5,1024]{3,0,2,1:T(2,128)(2,1)}, u32[]{:S(2)}) copy-start(bf16[2,5,5,1024]{3,0,2,1:T(2,128)(2,1)} %param.28) | copy-start | bytes 307204
  61.5 0.7 copy-start.2
  64.2 85.9 %collective-permute-start = (f32[5,1024]{1,0:T(8,128)}, f32[5,1024]{1,0:T(8,128)}, u32[]{:S(2)}, u32[]{:S(2)}) collective-permute-start(f32[5,1024]{1,0:T(8,128)} %bitcast.118), channel_id=1, source_target_pairs={{0,1},{1,2},{2,3},{3,4},{4,5},{5,6},{6,7},{7,8},{8,9},{9,10},{10,1... | collective-permute-start | bytes 61448 | tf_op jit(solution)/shard_map/ppermute | solution.py:16
  66.7 5.5 %copy-start.8 = (s32[128]{0:T(128)S(1)}, s32[128]{0:T(128)}, u32[]{:S(2)}) copy-start(s32[128]{0:T(128)} %param.31) | copy-start | bytes 1540
  66.8 84.1 %collective-permute-start.1 = (f32[5,1024]{1,0:T(8,128)}, f32[5,1024]{1,0:T(8,128)}, u32[]{:S(2)}, u32[]{:S(2)}) collective-permute-start(f32[5,1024]{1,0:T(8,128)} %bitcast.119), channel_id=1, source_target_pairs={{1,0},{2,1},{3,2},{4,3},{5,4},{6,5},{7,6},{8,7},{9,8},{10,9},{11,1... | collective-permute-start | bytes 61448 | tf_op jit(solution)/shard_map/ppermute | solution.py:16
  76.3 11.5 %collective-permute-start.4 = (bf16[34,16,1]{0,1,2:T(8,128)(2,1)S(1)}, bf16[34,16,1]{0,1,2:T(8,128)(2,1)S(1)}, u32[]{:S(2)}, u32[]{:S(2)}) collective-permute-start(bf16[34,16,1]{0,1,2:T(8,128)(2,1)S(1)} %get-tuple-element.169), channel_id=1, source_target_pairs={{0,4},{1,5},{2,6},{3,7},{8,12},{9,13},{10,14},{11,15},{16,20},{17,... | collective-permute-start | bytes 3272 | tf_op jit(solution)/shard_map/ppermute | solution.py:26
  77.6 10.2 %collective-permute-start.5 = (bf16[34,16,1]{0,1,2:T(8,128)(2,1)S(1)}, bf16[34,16,1]{0,1,2:T(8,128)(2,1)S(1)}, u32[]{:S(2)}, u32[]{:S(2)}) collective-permute-start(bf16[34,16,1]{0,1,2:T(8,128)(2,1)S(1)} %get-tuple-element.170), channel_id=1, source_target_pairs={{4,0},{5,1},{6,2},{7,3},{12,8},{13,9},{14,10},{15,11},{20,16},{21,... | collective-permute-start | bytes 3272 | tf_op jit(solution)/shard_map/ppermute | solution.py:27
  84.9 2.9 %copy-start.9 = (s32[128]{0:T(128)S(1)}, s32[128]{0:T(128)}, u32[]{:S(2)}) copy-start(s32[128]{0:T(128)} %param.34) | copy-start | bytes 1540
  88.7 60.1 %collective-permute-start.6 = (bf16[34,1,130]{0,1,2:T(2,128)(2,1)}, bf16[34,1,130]{0,1,2:T(2,128)(2,1)S(1)}, u32[]{:S(2)}, u32[]{:S(2)}) collective-permute-start(bf16[34,1,130]{0,1,2:T(2,128)(2,1)} %get-tuple-element.167), channel_id=1, source_target_pairs={{0,1},{1,2},{2,3},{4,5},{5,6},{6,7},{8,9},{9,10},{10,11},{12,13},{... | collective-permute-start | bytes 26528 | tf_op jit(solution)/shard_map/ppermute | solution.py:26
  90.6 58.2 %collective-permute-start.7 = (bf16[34,1,130]{0,1,2:T(2,128)(2,1)}, bf16[34,1,130]{0,1,2:T(2,128)(2,1)}, u32[]{:S(2)}, u32[]{:S(2)}) collective-permute-start(bf16[34,1,130]{0,1,2:T(2,128)(2,1)} %get-tuple-element.168), channel_id=1, source_target_pairs={{1,0},{2,1},{3,2},{5,4},{6,5},{7,6},{9,8},{10,9},{11,10},{13,12},{... | collective-permute-start | bytes 26528 | tf_op jit(solution)/shard_map/ppermute | solution.py:27
  121.9 2.6 %copy-start.3 = (bf16[2,64,2,32]{3,2,1,0:T(2,128)(2,1)S(1)}, bf16[2,64,2,32]{3,2,1,0:T(2,128)(2,1)}, u32[]{:S(2)}) copy-start(bf16[2,64,2,32]{3,2,1,0:T(2,128)(2,1)} %get-tuple-element.106) | copy-start | bytes 49156
  121.9 2.7 %copy-start.7 = (s32[128]{0:T(128)S(1)}, s32[128]{0:T(128)}, u32[]{:S(2)}) copy-start(s32[128]{0:T(128)} %copy-done.6) | copy-start | bytes 1540
  121.9 8.0 %copy-start = (f32[32,16,128]{2,1,0:T(8,128)S(1)}, f32[32,16,128]{2,1,0:T(8,128)}, u32[]{:S(2)}) copy-start(f32[32,16,128]{2,1,0:T(8,128)} %param.36) | copy-start | bytes 786436
  121.9 9.4 %copy-start.5 = (f32[2,5,5]{2,0,1:T(2,128)S(1)}, f32[2,5,5]{2,0,1:T(2,128)}, u32[]{:S(2)}) copy-start(f32[2,5,5]{2,0,1:T(2,128)} %param.29) | copy-start | bytes 604
  131.3 29.8 %all-to-all-start = ((bf16[64,2,256]{2,1,0:T(2,128)(2,1)}), bf16[64,2,256]{2,1,0:T(2,128)(2,1)S(1)}, u32[]{:S(2)}, u32[]{:S(2)}) async-start(bf16[64,2,256]{2,1,0:T(2,128)(2,1)} %reshape.507), calls=%async_computation | async-start | bytes 131072 | tf_op jit(solution)/shard_map/all_to_all | solution.py:180
where the time goes:
time: 168 us; the launch traced here: 167 us
  starting transfers between devices  60.1 us (36%)
  local copies, waits for them, and re-layouts  44.4 us (26%)
  other arithmetic  37.3 us (22%)
  matrix products  15.8 us (9%)
  waiting for transfers between devices  8.53 us (5%)
    all_to_all x1, starting transfers between devices, shards(): lax.all_to_all(slot_send, 'mer', split_axis=0, concat_axis=0, tiled=True)  20.4 us
    gather x2, local copies, waits for them, and re-layouts, one_block(): table = sample_rows[part_starts[:, None] + offsets[None, :]]  19.3 us
    all_to_all x1, starting transfers between devices, shards(): lax.all_to_all(value_send, 'mer', split_axis=0, concat_axis=0, tiled=True)  15.3 us
    unnamed x33, local copies, waits for them, and re-layouts  11.3 us
    ppermute x3, starting transfers between devices, padded_2(): after = lax.ppermute(first, axis, down)  11 us
    cos x1, other arithmetic, azimuth_tables(): cosine = jnp.cos(angles)  9.18 us
    another operation x2, other arithmetic  8.83 us
    all_to_all x1, waiting for transfers between devices, shards(): lax.all_to_all(value_send, 'mer', split_axis=0, concat_axis=0, tiled=True)  8.5 us
  transfers between devices with their start and end apart: 10, of which 1 were waited for; matrix products, arithmetic and copies ran while one was open for 53% of the time, Pallas kernels for 0%

commit v1 on v0

v1 whole, which is shorter than its diff:
```python
import functools
import math

import jax
import jax.numpy as jnp
import ml_dtypes
import numpy as np
from jax import lax
from jax.experimental import pallas as pl
from jax.experimental.pallas import tpu as pltpu
from jax.sharding import PartitionSpec as P

MESH = pl.DeviceIdType.MESH
F32 = jnp.float32
BF16 = jnp.bfloat16
NZ_FULL = 16
NREC = 128
RP = 64


def gll_derivative():
    nodes = np.array([-1.0, -math.sqrt(3.0 / 7.0), 0.0, math.sqrt(3.0 / 7.0), 1.0])
    legendre = (35.0 * nodes**4 - 30.0 * nodes**2 + 3.0) / 8.0
    table = np.zeros((5, 5))
    for i in range(5):
        for j in range(5):
            if i != j:
                table[i, j] = legendre[i] / (legendre[j] * (nodes[i] - nodes[j]))
    table[0, 0] = -5.0
    table[4, 4] = 5.0
    return table.astype(np.float32)


def split_bf16(matrix):
    hi = matrix.astype(ml_dtypes.bfloat16)
    lo = (matrix - hi.astype(np.float32)).astype(ml_dtypes.bfloat16)
    return hi, lo


def constants():
    order = np.arange(512)
    sample = np.arange(1024)
    angle = (order[:, None] * sample[None, :] % 1024) * (2.0 * math.pi / 1024)
    weight = np.where(order == 0, 1.0, 2.0)[:, None]
    synthesis = np.concatenate([weight * np.cos(angle), -weight * np.sin(angle)], 0)
    analysis = np.concatenate([np.cos(angle), -np.sin(angle)], 0).T / 1024
    synthesis = synthesis.astype(np.float32).astype(ml_dtypes.bfloat16)
    analysis = analysis.astype(np.float32).astype(ml_dtypes.bfloat16)
    deriv = gll_derivative()
    eye5, eye2 = np.eye(5, dtype=np.float32), np.eye(2, dtype=np.float32)
    d1 = np.zeros((RP, RP), np.float32)
    d2 = np.zeros((RP, RP), np.float32)
    d1[:50, :50] = np.kron(np.kron(deriv, eye5), eye2)
    d2[:50, :50] = np.kron(np.kron(eye5, deriv), eye2)
    h1, l1 = split_bf16(d1)
    h2, l2 = split_bf16(d2)
    grad = np.concatenate(
        [np.concatenate([h1, h1, l1], 1), np.concatenate([h2, h2, l2], 1)], 0
    )
    h1, l1, h2, l2 = h1.T, l1.T, h2.T, l2.T
    div = np.concatenate([h1, h2, h1, h2, l1, l2], 1)
    return synthesis[:, :512], analysis, grad, div


def dot(a, b):
    return jnp.dot(a, b, preferred_element_type=F32)


def kernel(
    ny, nz, nb,
    disp_h, rad_h, mod_h, imass_h, cnt_h, sp_h, ro_h, fs_h, ws_h, box_h, speed_h, tsyn_h, tana_h, grad_h, div_h,
    ga_h, ba_h,
    disp, rad, mod, imass, cnt, sp, ro, fs, ws, box, speed, tsyn, tana, gradm, divm,
    field, modf, radf, massf, lhs1, lhs2, pots, tracs, gather, divs, ga,
    meta, edge, edge_in, xin, yout, yin, zout, zin, vals, rhs, route, face, face_in, acc,
    in_sem, out_sem, send_sem, recv_sem,
):
    mer = lax.axis_index("mer")
    grp = lax.axis_index("grp")
    bx = lax.axis_index("box")
    my_y = mer // nz
    my_z = mer % nz
    n_mer = ny * nz
    chain = (mer * 2 + grp) * nb + bx
    n_dev = n_mer * 2 * nb

    def chain_id(d):
        d = (d + n_dev) % n_dev
        return (d // (2 * nb), (d // nb) % 2, d % nb)

    mer_up = ((mer + 1) % n_mer, grp, bx)
    mer_down = ((mer + n_mer - 1) % n_mer, grp, bx)
    box_up = (mer, grp, (bx + 1) % nb)
    box_down = (mer, grp, (bx + nb - 1) % nb)
    other = (mer, 1 - grp, bx)
    next_id = chain_id(chain + 1)
    prev_id = chain_id(chain - 1)
    y_peers = [(((my_y + k) % ny) * nz + my_z, grp, bx) for k in range(1, ny)]
    z_peers = [(my_y * nz + (my_z + k) % nz, grp, bx) for k in range(1, nz)]
    partners = [mer_up, mer_down, box_up, box_down, other, next_id, prev_id] + y_peers + z_peers

    loads = []
    for index, (src, dst) in enumerate(
        [
            (disp_h, disp), (cnt_h, cnt), (rad_h, rad), (grad_h, gradm), (tsyn_h, tsyn), (mod_h, mod), (sp_h, sp),
            (ws_h, ws), (ro_h, ro), (fs_h, fs), (box_h, box), (tana_h, tana), (div_h, divm), (speed_h, speed),
            (imass_h, imass),
        ]
    ):
        copy = pltpu.make_async_copy(src, dst, in_sem.at[index])
        copy.start()
        loads.append(copy)
    (l_disp, l_cnt, l_rad, l_grad, l_tsyn, l_mod, l_sp, l_ws, l_ro, l_fs, l_box, l_tana, l_div, l_speed, l_imass) = loads

    barrier = pltpu.get_barrier_semaphore()
    for partner in partners:
        pl.semaphore_signal(barrier, inc=1, device_id=partner, device_id_type=MESH)

    counter = [0]

    def remote(src, dst, partner):
        index = counter[0]
        counter[0] += 1
        copy = pltpu.make_async_remote_copy(
            src_ref=src, dst_ref=dst, send_sem=send_sem.at[index], recv_sem=recv_sem.at[index],
            device_id=partner, device_id_type=MESH,
        )
        copy.start()
        return copy

    lane = lax.broadcasted_iota(jnp.int32, (1, 1024), 1)
    order = lane & 511
    orderf = order.astype(F32)
    sign = (1 - 2 * (order & 1)).astype(BF16)
    row64 = lax.broadcasted_iota(jnp.int32, (RP, 1), 0)

    field[48:RP, :] = jnp.zeros((RP - 48, 1024), F32)
    radf[...] = jnp.ones((RP, 128), F32)
    l_disp.wait()
    for i in range(25):
        field[2 * i : 2 * i + 2, :] = disp[i]
    l_cnt.wait()
    counts = jnp.where((row64 & 1) == 0, cnt[0:1, 0:1], cnt[0:1, 1:2])
    mask = (order < counts).astype(F32)
    f = field[...] * mask
    l_rad.wait()
    for i in range(25):
        radf[2 * i : 2 * i + 2, :] = jnp.broadcast_to(rad[i // 5][:, i % 5 : i % 5 + 1], (2, 128))
    invr = (1.0 / radf[...])[:, 0:1]
    fhi = f.astype(BF16)
    flo = (f - fhi.astype(F32)).astype(BF16)
    l_grad.wait()
    g12 = dot(gradm[...], jnp.concatenate([fhi, flo, fhi], 0)).astype(BF16)
    lhs1[0:128, :] = g12
    lhs1[256:384, :] = g12 * sign
    g3 = (jnp.concatenate([-f[:, 512:], f[:, :512]], 1) * orderf * invr).astype(BF16)
    lhs1[128:192, :] = g3
    lhs1[384:448, :] = g3 * sign
    lhs1[192:256, :] = fhi
    lhs1[448:512, :] = fhi * sign

    l_sp.wait()
    l_ws.wait()
    second = (sp[...] >= 25).astype(jnp.int32)
    point = (sp[...] - 25 * second) * 2 + second
    packed = ((ws[...] >> 7) * RP + point) | ((ws[...] & 127) << 9)
    packed = jnp.broadcast_to(packed, (128, 128)).T
    key = packed & 511
    offset = packed >> 9
    lane128 = lax.broadcasted_iota(jnp.int32, (128, 128), 1)
    for t in range(4):
        cols = slice(t * 128, (t + 1) * 128)
        gather[0:128, cols] = (key == lane128 + t * 128).astype(F32).astype(BF16)
        gather[128:256, cols] = (key + RP == lane128 + t * 128).astype(F32).astype(BF16)

    modf[48:RP, :] = jnp.zeros((RP - 48, 1024), F32)
    l_mod.wait()
    for i in range(25):
        modf[2 * i : 2 * i + 2, :] = mod[i].astype(F32)
    l_tsyn.wait()
    for s in range(2):
        half = slice(s * 512, (s + 1) * 512)
        phys = dot(lhs1[s * 256 : (s + 1) * 256, :], tsyn[...])
        for c in range(3):
            lhs2[c * RP : (c + 1) * RP, half] = (modf[:, half] * phys[c * RP : (c + 1) * RP]).astype(BF16)
        for t in range(4):
            b = s * 4 + t
            pots[b * RP : (b + 1) * RP, :] = phys[192:256, t * 128 : (t + 1) * 128].astype(BF16)

    l_box.wait()
    yout[0:32, :] = box[pl.ds(0, 32, stride=16), :]
    yout[32:64, :] = box[pl.ds(15, 32, stride=16), :]
    far_lane = 127 * (1 - grp)
    near_lane = 127 * grp
    row128 = lax.broadcasted_iota(jnp.int32, (128, 128), 0)
    pick = (row128 == far_lane).astype(F32).astype(BF16)
    column = dot(box[...].astype(BF16), pick).reshape(64, 8, 128)
    block64 = lax.broadcasted_iota(jnp.int32, (64, 1, 128), 0)
    lane64 = lax.broadcasted_iota(jnp.int32, (64, 1, 128), 2)
    place = (block64 >> 1) + (block64 & 1) * 64
    pot_mask = lane64 == place
    trac_mask = lane64 == place + 32
    zout[...] = jnp.sum(jnp.where(pot_mask, column, 0.0), axis=0)
    l_ro.wait()
    l_fs.wait()
    meta[0] = jnp.broadcast_to(ro[...] * 16 + fs[...], (8, 128))

    pl.semaphore_wait(barrier, len(partners))
    meta_copies = [remote(meta.at[0], meta.at[k + 1], y_peers[k]) for k in range(ny - 1)]
    x_copies = [
        remote(box.at[pl.ds(0, 16)], xin.at[1], mer_down),
        remote(box.at[pl.ds(496, 16)], xin.at[0], mer_up),
    ]
    y_copies = [
        remote(yout.at[pl.ds(0, 32)], yin.at[1], box_down),
        remote(yout.at[pl.ds(32, 32)], yin.at[0], box_up),
    ]
    z_copy = remote(zout, zin, other)

    l_tana.wait()
    coeffs = dot(lhs2[...], tana[...])
    c1, c2, c3 = coeffs[0:64] * mask, coeffs[64:128] * mask, coeffs[128:192] * mask

    c2hi = c2.astype(BF16)
    synth = dot(jnp.concatenate([c2hi, c2hi * sign], 0), tsyn[...]).astype(BF16)
    for s in range(2):
        for t in range(4):
            b = s * 4 + t
            tracs[b * RP : (b + 1) * RP, :] = synth[s * RP : (s + 1) * RP, t * 128 : (t + 1) * 128]
    windows = []
    for table in (pots, tracs):
        got = dot(gather[...], table[...])
        windows.append(jnp.where(lane128 >= offset, got[0:128], got[128:256]))
    where = (offset + (lane128 & 31)) & 127
    pieces = []
    for h in range(2):
        rows = slice(h * 64, (h + 1) * 64)
        for window in windows:
            pieces.append(jnp.take_along_axis(window[rows], where[rows], axis=1, mode="promise_in_bounds"))
    quarter = lane128[0:64] >> 5
    merged = jnp.where(
        quarter == 0, pieces[0], jnp.where(quarter == 1, pieces[1], jnp.where(quarter == 2, pieces[2], pieces[3]))
    )
    vals[0] = merged.astype(BF16)
    val_copies = [remote(vals.at[0], vals.at[k + 1], y_peers[k]) for k in range(ny - 1)]

    c1hi = c1.astype(BF16)
    c1lo = (c1 - c1hi.astype(F32)).astype(BF16)
    c2lo = (c2 - c2hi.astype(F32)).astype(BF16)
    l_div.wait()
    div = dot(divm[...], jnp.concatenate([c1hi, c2hi, c1lo, c2lo, c1hi, c2hi], 0))
    div = div + jnp.concatenate([c3[:, 512:], -c3[:, :512]], 1) * orderf * invr
    divs[...] = div
    for k in range(5):
        edge[0, k : k + 1, :] = divs[41 + 2 * k : 42 + 2 * k, :]
        edge[1, k : k + 1, :] = divs[2 * k : 2 * k + 1, :]
    edge[0, 5:8, :] = jnp.zeros((3, 1024), F32)
    edge[1, 5:8, :] = jnp.zeros((3, 1024), F32)
    edge_copies = [
        remote(edge.at[0], edge_in.at[0], next_id),
        remote(edge.at[1], edge_in.at[1], prev_id),
    ]

    for copy in meta_copies:
        copy.wait_recv()
    trow = lax.broadcasted_iota(jnp.int32, (nz * 8, 128), 0)
    target = (my_y * nz + (my_z + (trow >> 3)) % nz) * 16 + (trow & 7)
    for k in range(ny):
        cols = slice(k * 128, (k + 1) * 128)
        keys = jnp.broadcast_to(meta[k][0:1, :], (nz * 8, 128))
        route[0 : nz * 8, cols] = (keys == target).astype(F32).astype(BF16)
        route[nz * 8 : nz * 16, cols] = (pltpu.roll(keys, 64, 1) == target + 8).astype(F32).astype(BF16)

    l_speed.wait()
    b = box[...]
    row512 = lax.broadcasted_iota(jnp.int32, (512, 128), 0) & 15
    lane512 = lax.broadcasted_iota(jnp.int32, (512, 128), 1)
    zero16 = jnp.zeros((16, 128), F32)
    total = jnp.concatenate([zero16, b[:-16]], 0) + jnp.concatenate([b[16:], zero16], 0)
    total = total + jnp.where(row512 == 0, 0.0, pltpu.roll(b, 1, 0)) + jnp.where(row512 == 15, 0.0, pltpu.roll(b, 511, 0))
    total = total + jnp.where(lane512 == 0, 0.0, pltpu.roll(b, 1, 1)) + jnp.where(lane512 == 127, 0.0, pltpu.roll(b, 127, 1))
    acc[...] = speed[...] * (total - 6.0 * b)

    for copy in val_copies:
        copy.wait_recv()
    for k in range(ny):
        v = vals[k].astype(F32)
        rhs[k * 128 : k * 128 + 64, :] = vals[k]
        rhs[k * 128 + 64 : (k + 1) * 128, :] = pltpu.roll(v, 64, 1).astype(BF16)
    routed = dot(route[...], rhs[...])
    face[...] = jnp.where(
        lax.broadcasted_iota(jnp.int32, (nz * 8, 128), 1) < 64, routed[: nz * 8], routed[nz * 8 :]
    ).reshape(nz, 8, 128)
    face_copies = [remote(face.at[k + 1], face_in.at[k], z_peers[k]) for k in range(nz - 1)]

    for copy in x_copies + y_copies + [z_copy]:
        copy.wait_recv()
    acc[0:16, :] += speed[0:16, :] * jnp.where(mer == 0, 0.0, xin[0])
    acc[496:512, :] += speed[496:512, :] * jnp.where(mer == n_mer - 1, 0.0, xin[1])
    acc[pl.ds(0, 32, stride=16), :] += speed[pl.ds(0, 32, stride=16), :] * jnp.where(bx == 0, 0.0, yin[0])
    acc[pl.ds(15, 32, stride=16), :] += speed[pl.ds(15, 32, stride=16), :] * jnp.where(bx == nb - 1, 0.0, yin[1])
    lane128 = lax.broadcasted_iota(jnp.int32, (128, 128), 1)
    far = (lane128 == far_lane).astype(F32).astype(BF16)
    near = (lane128 == near_lane).astype(F32).astype(BF16)
    spread = jnp.where(pot_mask, zin[...][None], 0.0).reshape(512, 128)
    acc[...] += speed[...] * dot(spread.astype(BF16), far)

    l_imass.wait()
    for i in range(25):
        massf[2 * i : 2 * i + 2, :] = jnp.broadcast_to(imass[i // 5][:, i % 5 : i % 5 + 1], (2, 128))
    for copy in edge_copies:
        copy.wait_recv()
    for k in range(5):
        inner = divs[40 + 2 * k : 41 + 2 * k, :] + divs[1 + 2 * k : 2 + 2 * k, :]
        divs[40 + 2 * k : 41 + 2 * k, :] = inner
        divs[1 + 2 * k : 2 + 2 * k, :] = inner
        divs[2 * k : 2 * k + 1, :] += jnp.where(chain == 0, 0.0, edge_in[0, k : k + 1, :])
        divs[41 + 2 * k : 42 + 2 * k, :] += jnp.where(chain == n_dev - 1, 0.0, edge_in[1, k : k + 1, :])
    for i in range(25):
        ga[i] = divs[2 * i : 2 * i + 2, :] * -massf[2 * i : 2 * i + 2, 0:1]
    ga_copy = pltpu.make_async_copy(ga, ga_h, out_sem.at[0])
    ga_copy.start()

    for copy in face_copies:
        copy.wait_recv()
    mine = face[0]
    mine = mine + jnp.sum(face_in[...], axis=0)

    def spread_face(mask):
        part = jnp.where(mask, mine[None], 0.0).reshape(512, 128)
        hi = part.astype(BF16)
        lo = (part - hi.astype(F32)).astype(BF16)
        return dot(jnp.concatenate([hi, lo], 1), jnp.concatenate([near, near], 0))

    acc[...] += speed[...] * spread_face(pot_mask) + 0.25 * spread_face(trac_mask)
    ba_copy = pltpu.make_async_copy(acc, ba_h, out_sem.at[1])
    ba_copy.start()
    for copy in meta_copies + x_copies + y_copies + [z_copy] + val_copies + edge_copies + face_copies:
        copy.wait_send()
    ga_copy.wait()
    ba_copy.wait()


def shards(ny, nz, nb, displacement, radius, bulk, imass, counts, source, owner, slot, window, box, speed):
    tsyn, tana, grad, div = constants()
    args = [
        displacement.transpose(1, 2, 0, 3).reshape(25, 2, 1024),
        radius.transpose(1, 0, 2),
        bulk.transpose(1, 2, 0, 3).reshape(25, 2, 1024),
        imass.transpose(1, 0, 2),
        counts.reshape(1, 2),
        source.reshape(1, NREC),
        owner.reshape(1, NREC),
        slot.reshape(1, NREC),
        window.reshape(1, NREC),
        box.reshape(512, 128),
        speed.reshape(512, 128),
        jnp.asarray(tsyn), jnp.asarray(tana), jnp.asarray(grad), jnp.asarray(div),
    ]
    n_copies = 2 * (ny - 1) + 5 + 2 + nz - 1
    hbm = pl.BlockSpec(memory_space=pltpu.HBM)
    vmem = pltpu.VMEM
    scratch = [vmem(a.shape, a.dtype) for a in args] + [
        vmem((RP, 1024), F32),
        vmem((RP, 1024), F32),
        vmem((RP, 128), F32),
        vmem((RP, 128), F32),
        vmem((512, 1024), BF16),
        vmem((192, 1024), BF16),
        vmem((512, 128), BF16),
        vmem((512, 128), BF16),
        vmem((256, 512), BF16),
        vmem((RP, 1024), F32),
        vmem((25, 2, 1024), F32),
        vmem((ny, 8, 128), jnp.int32),
        vmem((2, 8, 1024), F32),
        vmem((2, 8, 1024), F32),
        vmem((2, 16, 128), F32),
        vmem((64, 128), F32),
        vmem((2, 32, 128), F32),
        vmem((8, 128), F32),
        vmem((8, 128), F32),
        vmem((ny, 64, 128), BF16),
        vmem((ny * 128, 128), BF16),
        vmem((nz * 16, ny * 128), BF16),
        vmem((nz, 8, 128), F32),
        vmem((nz - 1, 8, 128), F32),
        vmem((512, 128), F32),
        pltpu.SemaphoreType.DMA((15,)),
        pltpu.SemaphoreType.DMA((2,)),
        pltpu.SemaphoreType.DMA((n_copies,)),
        pltpu.SemaphoreType.DMA((n_copies,)),
    ]
    ga, ba = pl.pallas_call(
        functools.partial(kernel, ny, nz, nb),
        out_shape=(jax.ShapeDtypeStruct((25, 2, 1024), F32), jax.ShapeDtypeStruct((512, 128), F32)),
        in_specs=[hbm] * len(args),
        out_specs=(hbm, hbm),
        scratch_shapes=scratch,
        compiler_params=pltpu.CompilerParams(
            collective_id=0, has_side_effects=True, vmem_limit_bytes=60 * 2**20
        ),
        name="step",
    )(*args)
    ga = ga.reshape(5, 5, 2, 1024).transpose(2, 0, 1, 3)
    return ga, ba.reshape(32, 16, 128)


def solution(mesh):
    n_mer = mesh.shape["mer"]
    nz = NZ_FULL if n_mer == 64 else 2
    d = P(("mer", "grp", "box"))
    return jax.shard_map(
        functools.partial(shards, n_mer // nz, nz, mesh.shape["box"]),
        mesh=mesh,
        in_specs=(d, d, d, d, d, d, d, d, d, P("mer", "box", "grp"), P("mer", "box", "grp")),
        out_specs=(d, P("mer", "box", "grp")),
        check_vma=False,
    )
```

time: 168 us -> 32.8 us (0.20)
  starting transfers between devices: 60.1 us -> 0 us
  local copies, waits for them, and re-layouts: 44.4 us -> 3.29 us
  other arithmetic: 37.3 us -> 0 us
  Pallas kernels: 0 us -> 28.6 us
  matrix products: 15.8 us -> 0 us
  waiting for transfers between devices: 8.53 us -> 0 us
    all_to_all x2 -> x0, starting transfers between devices: 35.7 us -> none  [the longest x1 20.4 us: shards(): lax.all_to_all(slot_send, 'mer', split_axis=0, concat_axis=0, tiled=True)]
    pallas_call x0 -> x1, Pallas kernels: none -> 28.6 us  [shards(): pl.pallas_call(functools.partial(kernel, ny, nz, nb), out_shape=(jax.Shap...]
    ppermute x8 -> x0, starting transfers between devices: 24.4 us -> none  [the longest x3 11 us: padded_2(): after = lax.ppermute(first, axis, down)]
    gather x4 -> x0, local copies, waits for them, and re-layouts: 21 us -> none  [the longest x2 19.3 us: one_block(): table = sample_rows[part_starts[:, None] + offsets[None, :]]]
    dot_general x8 -> x0, matrix products: 15.8 us -> none  [the longest x2 8 us: one_block(): jnp.einsum('bik,bjk->bij', part_coeffs, table, preferred_element_type=jnp...]
    another operation x5 -> x0, other arithmetic: 11.4 us -> none
    cos x1 -> x0, other arithmetic: 9.18 us -> none  [azimuth_tables(): cosine = jnp.cos(angles)]
    all_to_all x2 -> x0, waiting for transfers between devices: 8.5 us -> none  [the longest x1 8.5 us: shards(): lax.all_to_all(value_send, 'mer', split_axis=0, concat_axis=0, tiled=True)]
  transfers between devices with their start and end apart: 10 -> 0, of which waited for: 1 -> 0; matrix products, arithmetic and copies ran while one was open for 53% -> 0% of each run, Pallas kernels for 0% -> 0%
where the time goes in v1:
time: 32.8 us; the launch traced here: 32.6 us
  Pallas kernels  28.6 us (87%)
  local copies, waits for them, and re-layouts  3.29 us (10%)
  between operations  0.64 us (2%)
    pallas_call x1, Pallas kernels, shards(): pl.pallas_call(functools.partial(kernel, ny, nz, nb), out_shape=(jax.Shap...  28.6 us
    unnamed x2, local copies, waits for them, and re-layouts  3.29 us

profile of v1, /device:TPU:6, one launch (start us, length us, event | category | flops | bytes accessed | tf_op | source)
XLA Modules:
  0.0 32.6 jit_solution(17199181153340378453)
XLA Ops:
  0.6 28.6 %step.1 = (f32[25,2,1024]{2,1,0:T(2,128)}, f32[512,128]{1,0:T(8,128)}) custom-call(f32[25,2,1024]{2,1,0:T(2,128)} %bitcast.23, f32[5,2,5]{2,1,0:T(2,128)} %bitcast.25, bf16[25,2,1024]{2,1,0:T(2,128)(2,1)} %bitcast.24, f32[5,2,5]{2,1,0:T(2,128)} %bitcast.26, s32[1,2]{1,0:T(1,128)} %bitcast.27, s32[1,128]{1,0:T(1,128)} %bitcast.28, s32[1,128]{1,0:T(1,128)} %bitcast.29, ...), custom_call_target="tpu_custom_call" | custom-call | tf_op jit(solution)/shard_map/step/pallas_call | solution.py:394
  29.3 1.6 %copy.19 = f32[2,5,5,1024]{3,0,2,1:T(2,128)} copy(f32[2,5,5,1024]{3,0,2,1:T(2,128)} %bitcast.22) | data formatting | bytes 409600
  30.9 1.7 %copy.20 = f32[32,16,128]{2,1,0:T(8,128)} copy(f32[32,16,128]{2,1,0:T(8,128)} %bitcast.21) | data formatting | bytes 524288

commit v2 on v1

--- a/solution.py
+++ b/solution.py
@@ -69,11 +69,11 @@
 def kernel(
     ny, nz, nb,
     disp_h, rad_h, mod_h, imass_h, cnt_h, sp_h, ro_h, fs_h, ws_h, box_h, speed_h, tsyn_h, tana_h, grad_h, div_h,
-    ga_h, ba_h,
+    ga, acc,
     disp, rad, mod, imass, cnt, sp, ro, fs, ws, box, speed, tsyn, tana, gradm, divm,
-    field, modf, radf, massf, lhs1, lhs2, pots, tracs, gather, divs, ga,
-    meta, edge, edge_in, xin, yout, yin, zout, zin, vals, rhs, route, face, face_in, acc,
-    in_sem, out_sem, send_sem, recv_sem,
+    field, modf, radf, massf, lhs1, lhs2, pots, tracs, gather, divs,
+    edge, edge_in, xin, yout, yin, zout, zin, vals, route, face, face_in,
+    in_sem, send_sem, recv_sem,
 ):
     mer = lax.axis_index("mer")
     grp = lax.axis_index("grp")
@@ -95,9 +95,16 @@
     other = (mer, 1 - grp, bx)
     next_id = chain_id(chain + 1)
     prev_id = chain_id(chain - 1)
-    y_peers = [(((my_y + k) % ny) * nz + my_z, grp, bx) for k in range(1, ny)]
-    z_peers = [(my_y * nz + (my_z + k) % nz, grp, bx) for k in range(1, nz)]
-    partners = [mer_up, mer_down, box_up, box_down, other, next_id, prev_id] + y_peers + z_peers
+    ahead = sorted(
+        [(dy, dz) for dy in range(ny) for dz in range(nz) if dy or dz],
+        key=lambda step: (-min(step[1], nz - step[1]) - min(step[0], ny - step[0]), step),
+    )
+    owners = [(((my_y + dy) % ny) * nz + (my_z + dz) % nz, grp, bx) for dy, dz in ahead]
+    partners = owners + [mer_up, mer_down, box_up, box_down, other, next_id, prev_id]
+
+    barrier = pltpu.get_barrier_semaphore()
+    for partner in partners:
+        pl.semaphore_signal(barrier, inc=1, device_id=partner, device_id_type=MESH)
 
     loads = []
     for index, (src, dst) in enumerate(
@@ -111,10 +118,6 @@
         copy.start()
         loads.append(copy)
     (l_disp, l_cnt, l_rad, l_grad, l_tsyn, l_mod, l_sp, l_ws, l_ro, l_fs, l_box, l_tana, l_div, l_speed, l_imass) = loads
-
-    barrier = pltpu.get_barrier_semaphore()
-    for partner in partners:
-        pl.semaphore_signal(barrier, inc=1, device_id=partner, device_id_type=MESH)
 
     counter = [0]
 
@@ -173,6 +176,15 @@
         gather[0:128, cols] = (key == lane128 + t * 128).astype(F32).astype(BF16)
         gather[128:256, cols] = (key + RP == lane128 + t * 128).astype(F32).astype(BF16)
 
+    l_ro.wait()
+    l_fs.wait()
+    row = lax.broadcasted_iota(jnp.int32, (ny * nz * 8, 128), 0)
+    step = row >> 3
+    target = (((my_y + step // nz) % ny) * nz + (my_z + step % nz) % nz) * 16 + (row & 7)
+    keys = jnp.broadcast_to(ro[...] * 16 + fs[...], (ny * nz * 8, 128))
+    route[:, 0:128] = (keys == target).astype(F32).astype(BF16)
+    route[:, 128:256] = (keys == target + 8).astype(F32).astype(BF16)
+
     modf[48:RP, :] = jnp.zeros((RP - 48, 1024), F32)
     l_mod.wait()
     for i in range(25):
@@ -201,22 +213,6 @@
     pot_mask = lane64 == place
     trac_mask = lane64 == place + 32
     zout[...] = jnp.sum(jnp.where(pot_mask, column, 0.0), axis=0)
-    l_ro.wait()
-    l_fs.wait()
-    meta[0] = jnp.broadcast_to(ro[...] * 16 + fs[...], (8, 128))
-
-    pl.semaphore_wait(barrier, len(partners))
-    meta_copies = [remote(meta.at[0], meta.at[k + 1], y_peers[k]) for k in range(ny - 1)]
-    x_copies = [
-        remote(box.at[pl.ds(0, 16)], xin.at[1], mer_down),
-        remote(box.at[pl.ds(496, 16)], xin.at[0], mer_up),
-    ]
-    y_copies = [
-        remote(yout.at[pl.ds(0, 32)], yin.at[1], box_down),
-        remote(yout.at[pl.ds(32, 32)], yin.at[0], box_up),
-    ]
-    z_copy = remote(zout, zin, other)
-
     l_tana.wait()
     coeffs = dot(lhs2[...], tana[...])
     c1, c2, c3 = coeffs[0:64] * mask, coeffs[64:128] * mask, coeffs[128:192] * mask
@@ -232,17 +228,24 @@
         got = dot(gather[...], table[...])
         windows.append(jnp.where(lane128 >= offset, got[0:128], got[128:256]))
     where = (offset + (lane128 & 31)) & 127
-    pieces = []
-    for h in range(2):
-        rows = slice(h * 64, (h + 1) * 64)
-        for window in windows:
-            pieces.append(jnp.take_along_axis(window[rows], where[rows], axis=1, mode="promise_in_bounds"))
-    quarter = lane128[0:64] >> 5
-    merged = jnp.where(
-        quarter == 0, pieces[0], jnp.where(quarter == 1, pieces[1], jnp.where(quarter == 2, pieces[2], pieces[3]))
-    )
-    vals[0] = merged.astype(BF16)
-    val_copies = [remote(vals.at[0], vals.at[k + 1], y_peers[k]) for k in range(ny - 1)]
+    pieces = [jnp.take_along_axis(window, where, axis=1, mode="promise_in_bounds") for window in windows]
+    merged = jnp.where((lane128 & 32) == 0, pieces[0], pieces[1])
+    vals[0:128, :] = jnp.where(lane128 < 64, merged, 0.0).astype(BF16)
+    vals[128:256, :] = jnp.where(lane128 < 64, 0.0, merged).astype(BF16)
+    face[...] = dot(route[...], vals[...]).reshape(ny * nz, 8, 128).astype(BF16)
+    pl.semaphore_wait(barrier, len(partners))
+    face_copies = [
+        remote(face.at[dy * nz + dz], face_in.at[k], owners[k]) for k, (dy, dz) in enumerate(ahead)
+    ]
+    x_copies = [
+        remote(box.at[pl.ds(0, 16)], xin.at[1], mer_down),
+        remote(box.at[pl.ds(496, 16)], xin.at[0], mer_up),
+    ]
+    y_copies = [
+        remote(yout.at[pl.ds(0, 32)], yin.at[1], box_down),
+        remote(yout.at[pl.ds(32, 32)], yin.at[0], box_up),
+    ]
+    z_copy = remote(zout, zin, other)
 
     c1hi = c1.astype(BF16)
     c1lo = (c1 - c1hi.astype(F32)).astype(BF16)
@@ -261,16 +264,6 @@
         remote(edge.at[1], edge_in.at[1], prev_id),
     ]
 
-    for copy in meta_copies:
-        copy.wait_recv()
-    trow = lax.broadcasted_iota(jnp.int32, (nz * 8, 128), 0)
-    target = (my_y * nz + (my_z + (trow >> 3)) % nz) * 16 + (trow & 7)
-    for k in range(ny):
-        cols = slice(k * 128, (k + 1) * 128)
-        keys = jnp.broadcast_to(meta[k][0:1, :], (nz * 8, 128))
-        route[0 : nz * 8, cols] = (keys == target).astype(F32).astype(BF16)
-        route[nz * 8 : nz * 16, cols] = (pltpu.roll(keys, 64, 1) == target + 8).astype(F32).astype(BF16)
-
     l_speed.wait()
     b = box[...]
     row512 = lax.broadcasted_iota(jnp.int32, (512, 128), 0) & 15
@@ -280,18 +273,6 @@
     total = total + jnp.where(row512 == 0, 0.0, pltpu.roll(b, 1, 0)) + jnp.where(row512 == 15, 0.0, pltpu.roll(b, 511, 0))
     total = total + jnp.where(lane512 == 0, 0.0, pltpu.roll(b, 1, 1)) + jnp.where(lane512 == 127, 0.0, pltpu.roll(b, 127, 1))
     acc[...] = speed[...] * (total - 6.0 * b)
-
-    for copy in val_copies:
-        copy.wait_recv()
-    for k in range(ny):
-        v = vals[k].astype(F32)
-        rhs[k * 128 : k * 128 + 64, :] = vals[k]
-        rhs[k * 128 + 64 : (k + 1) * 128, :] = pltpu.roll(v, 64, 1).astype(BF16)
-    routed = dot(route[...], rhs[...])
-    face[...] = jnp.where(
-        lax.broadcasted_iota(jnp.int32, (nz * 8, 128), 1) < 64, routed[: nz * 8], routed[nz * 8 :]
-    ).reshape(nz, 8, 128)
-    face_copies = [remote(face.at[k + 1], face_in.at[k], z_peers[k]) for k in range(nz - 1)]
 
     for copy in x_copies + y_copies + [z_copy]:
         copy.wait_recv()
@@ -318,13 +299,10 @@
         divs[41 + 2 * k : 42 + 2 * k, :] += jnp.where(chain == n_dev - 1, 0.0, edge_in[1, k : k + 1, :])
     for i in range(25):
         ga[i] = divs[2 * i : 2 * i + 2, :] * -massf[2 * i : 2 * i + 2, 0:1]
-    ga_copy = pltpu.make_async_copy(ga, ga_h, out_sem.at[0])
-    ga_copy.start()
 
     for copy in face_copies:
         copy.wait_recv()
-    mine = face[0]
-    mine = mine + jnp.sum(face_in[...], axis=0)
+    mine = face[0].astype(F32) + jnp.sum(face_in[...].astype(F32), axis=0)
 
     def spread_face(mask):
         part = jnp.where(mask, mine[None], 0.0).reshape(512, 128)
@@ -333,12 +311,16 @@
         return dot(jnp.concatenate([hi, lo], 1), jnp.concatenate([near, near], 0))
 
     acc[...] += speed[...] * spread_face(pot_mask) + 0.25 * spread_face(trac_mask)
-    ba_copy = pltpu.make_async_copy(acc, ba_h, out_sem.at[1])
-    ba_copy.start()
-    for copy in meta_copies + x_copies + y_copies + [z_copy] + val_copies + edge_copies + face_copies:
+    for copy in x_copies + y_copies + [z_copy] + edge_copies + face_copies:
         copy.wait_send()
-    ga_copy.wait()
-    ba_copy.wait()
+
+
+def write_out(ga, ba, ga_h, ba_h, sem):
+    copies = [pltpu.make_async_copy(ga, ga_h, sem.at[0]), pltpu.make_async_copy(ba, ba_h, sem.at[1])]
+    for copy in copies:
+        copy.start()
+    for copy in copies:
+        copy.wait()
 
 
 def shards(ny, nz, nb, displacement, radius, bulk, imass, counts, source, owner, slot, window, box, speed):
@@ -357,7 +339,7 @@
         speed.reshape(512, 128),
         jnp.asarray(tsyn), jnp.asarray(tana), jnp.asarray(grad), jnp.asarray(div),
     ]
-    n_copies = 2 * (ny - 1) + 5 + 2 + nz - 1
+    n_copies = 5 + 2 + ny * nz - 1
     hbm = pl.BlockSpec(memory_space=pltpu.HBM)
     vmem = pltpu.VMEM
     scratch = [vmem(a.shape, a.dtype) for a in args] + [
@@ -371,8 +353,6 @@
         vmem((512, 128), BF16),
         vmem((256, 512), BF16),
         vmem((RP, 1024), F32),
-        vmem((25, 2, 1024), F32),
-        vmem((ny, 8, 128), jnp.int32),
         vmem((2, 8, 1024), F32),
         vmem((2, 8, 1024), F32),
         vmem((2, 16, 128), F32),
@@ -380,28 +360,33 @@
         vmem((2, 32, 128), F32),
         vmem((8, 128), F32),
         vmem((8, 128), F32),
-        vmem((ny, 64, 128), BF16),
-        vmem((ny * 128, 128), BF16),
-        vmem((nz * 16, ny * 128), BF16),
-        vmem((nz, 8, 128), F32),
-        vmem((nz - 1, 8, 128), F32),
-        vmem((512, 128), F32),
+        vmem((256, 128), BF16),
+        vmem((ny * nz * 8, 256), BF16),
+        vmem((ny * nz, 8, 128), BF16),
+        vmem((ny * nz - 1, 8, 128), BF16),
         pltpu.SemaphoreType.DMA((15,)),
-        pltpu.SemaphoreType.DMA((2,)),
         pltpu.SemaphoreType.DMA((n_copies,)),
         pltpu.SemaphoreType.DMA((n_copies,)),
     ]
     ga, ba = pl.pallas_call(
         functools.partial(kernel, ny, nz, nb),
-        out_shape=(jax.ShapeDtypeStruct((25, 2, 1024), F32), jax.ShapeDtypeStruct((512, 128), F32)),
+        out_shape=(vmem((25, 2, 1024), F32), vmem((512, 128), F32)),
         in_specs=[hbm] * len(args),
-        out_specs=(hbm, hbm),
+        out_specs=(pl.BlockSpec(memory_space=vmem),) * 2,
         scratch_shapes=scratch,
         compiler_params=pltpu.CompilerParams(
-            collective_id=0, has_side_effects=True, vmem_limit_bytes=60 * 2**20
+            collective_id=0, has_side_effects=True, vmem_limit_bytes=40 * 2**20
         ),
         name="step",
-    )(*args)
+    )(*[pltpu.with_memory_space_constraint(a, pltpu.HBM) for a in args])
+    ga, ba = pl.pallas_call(
+        write_out,
+        out_shape=(jax.ShapeDtypeStruct((25, 2, 1024), F32), jax.ShapeDtypeStruct((512, 128), F32)),
+        in_specs=[pl.BlockSpec(memory_space=vmem)] * 2,
+        out_specs=(hbm, hbm),
+        scratch_shapes=[pltpu.SemaphoreType.DMA((2,))],
+        name="write_out",
+    )(pltpu.with_memory_space_constraint(ga, vmem), pltpu.with_memory_space_constraint(ba, vmem))
     ga = ga.reshape(5, 5, 2, 1024).transpose(2, 0, 1, 3)
     return ga, ba.reshape(32, 16, 128)
 

time: 32.8 us -> 30.1 us (0.918)
  the two profiles are of different devices: /device:TPU:6 before, /device:TPU:8 now
where the time goes in v2:
time: 30.1 us; the launch traced here: 30 us
  Pallas kernels  29.3 us (97%)
  between operations  0.64 us (2%)
    pallas_call x1, Pallas kernels, shards(): pl.pallas_call(functools.partial(kernel, ny, nz, nb), out_shape=(vmem((25...  28.6 us
    pallas_call x1, Pallas kernels, shards(): pl.pallas_call(write_out, out_shape=(jax.ShapeDtypeStruct((25, 2, 1024),...  0.79 us

profile of v2, /device:TPU:8, one launch (start us, length us, event | category | flops | bytes accessed | tf_op | source)
XLA Modules:
  0.0 30.0 jit_solution(10896536852047726849)
XLA Ops:
  0.6 28.6 %step.1 = (f32[25,2,1024]{2,1,0:T(2,128)S(1)}, f32[512,128]{1,0:T(8,128)S(1)}) custom-call(f32[25,2,1024]{2,1,0:T(2,128)} %bitcast.21, f32[5,2,5]{2,1,0:T(2,128)} %bitcast.23, bf16[25,2,1024]{2,1,0:T(2,128)(2,1)} %bitcast.22, f32[5,2,5]{2,1,0:T(2,128)} %bitcast.24, s32[1,2]{1,0:T(1,128)} %bitcast.25, s32[1,128]{1,0:T(1,128)} %bitcast.26, s32[1,128]{1,0:T(1,128)} %bitcast.27, ...), custom_call_target="tpu_custom_call" | custom-call | tf_op jit(solution)/shard_map/step/pallas_call | solution.py:371
  29.2 0.8 %write_out.1 = (f32[25,2,1024]{2,1,0:T(2,128)}, f32[512,128]{1,0:T(8,128)}) custom-call(f32[25,2,1024]{2,1,0:T(2,128)S(1)} %get-tuple-element.6.ga, f32[512,128]{1,0:T(8,128)S(1)} %get-tuple-element.7.ba), custom_call_target="tpu_custom_call" | custom-call | tf_op jit(solution)/shard_map/write_out/pallas_call | solution.py:382

commit v3 on v2

--- a/solution.py
+++ b/solution.py
@@ -72,8 +72,8 @@
     ga, acc,
     disp, rad, mod, imass, cnt, sp, ro, fs, ws, box, speed, tsyn, tana, gradm, divm,
     field, modf, radf, massf, lhs1, lhs2, pots, tracs, gather, divs,
-    edge, edge_in, xin, yout, yin, zout, zin, vals, route, face, face_in,
-    in_sem, send_sem, recv_sem,
+    edge, edge_in, xin, yout, yin, zout, zin, spot, vals, route, part_in, line, face, face_in,
+    in_sem, send_sem, recv_sem, relay_sem,
 ):
     mer = lax.axis_index("mer")
     grp = lax.axis_index("grp")
@@ -95,12 +95,15 @@
     other = (mer, 1 - grp, bx)
     next_id = chain_id(chain + 1)
     prev_id = chain_id(chain - 1)
-    ahead = sorted(
-        [(dy, dz) for dy in range(ny) for dz in range(nz) if dy or dz],
-        key=lambda step: (-min(step[1], nz - step[1]) - min(step[0], ny - step[0]), step),
-    )
-    owners = [(((my_y + dy) % ny) * nz + (my_z + dz) % nz, grp, bx) for dy, dz in ahead]
-    partners = owners + [mer_up, mer_down, box_up, box_down, other, next_id, prev_id]
+    y_ahead = sorted(range(1, ny), key=lambda k: (-min(k, ny - k), k))
+    z_ahead = sorted(range(1, nz), key=lambda k: (-min(k, nz - k), k))
+    y_peers = [(((my_y + k) % ny) * nz + my_z, grp, bx) for k in y_ahead]
+    z_peers = [(my_y * nz + (my_z + k) % nz, grp, bx) for k in z_ahead]
+    reach = nz // 4
+    relay_up = (my_y * nz + (my_z + reach) % nz, grp, bx)
+    relay_down = (my_y * nz + (my_z + nz - reach) % nz, grp, bx)
+    z_near = [z_peers[i] for i, k in enumerate(z_ahead) if min(k, nz - k) <= reach]
+    partners = z_near + y_peers + [mer_up, mer_down, box_up, box_down, other, next_id, prev_id]
 
     barrier = pltpu.get_barrier_semaphore()
     for partner in partners:
@@ -234,8 +237,10 @@
     vals[128:256, :] = jnp.where(lane128 < 64, 0.0, merged).astype(BF16)
     face[...] = dot(route[...], vals[...]).reshape(ny * nz, 8, 128).astype(BF16)
     pl.semaphore_wait(barrier, len(partners))
-    face_copies = [
-        remote(face.at[dy * nz + dz], face_in.at[k], owners[k]) for k, (dy, dz) in enumerate(ahead)
+    pl.semaphore_signal(relay_sem.at[0], inc=1, device_id=relay_up, device_id_type=MESH)
+    pl.semaphore_signal(relay_sem.at[1], inc=1, device_id=relay_down, device_id_type=MESH)
+    part_copies = [
+        remote(face.at[pl.ds(step * nz, nz)], part_in.at[k], y_peers[k]) for k, step in enumerate(y_ahead)
     ]
     x_copies = [
         remote(box.at[pl.ds(0, 16)], xin.at[1], mer_down),
@@ -274,6 +279,15 @@
     total = total + jnp.where(lane512 == 0, 0.0, pltpu.roll(b, 1, 1)) + jnp.where(lane512 == 127, 0.0, pltpu.roll(b, 127, 1))
     acc[...] = speed[...] * (total - 6.0 * b)
 
+    part = face[0:nz].astype(F32)
+    for k, copy in enumerate(part_copies):
+        copy.wait_recv()
+        part = part + part_in[k].astype(F32)
+    line[...] = part.astype(BF16)
+    pl.semaphore_wait(relay_sem.at[0], 1)
+    pl.semaphore_wait(relay_sem.at[1], 1)
+    face_copies = [remote(line.at[step], face_in.at[k], z_peers[k]) for k, step in enumerate(z_ahead)]
+
     for copy in x_copies + y_copies + [z_copy]:
         copy.wait_recv()
     acc[0:16, :] += speed[0:16, :] * jnp.where(mer == 0, 0.0, xin[0])
@@ -282,7 +296,6 @@
     acc[pl.ds(15, 32, stride=16), :] += speed[pl.ds(15, 32, stride=16), :] * jnp.where(bx == nb - 1, 0.0, yin[1])
     lane128 = lax.broadcasted_iota(jnp.int32, (128, 128), 1)
     far = (lane128 == far_lane).astype(F32).astype(BF16)
-    near = (lane128 == near_lane).astype(F32).astype(BF16)
     spread = jnp.where(pot_mask, zin[...][None], 0.0).reshape(512, 128)
     acc[...] += speed[...] * dot(spread.astype(BF16), far)
 
@@ -300,19 +313,26 @@
     for i in range(25):
         ga[i] = divs[2 * i : 2 * i + 2, :] * -massf[2 * i : 2 * i + 2, 0:1]
 
-    for copy in face_copies:
-        copy.wait_recv()
-    mine = face[0].astype(F32) + jnp.sum(face_in[...].astype(F32), axis=0)
-
-    def spread_face(mask):
-        part = jnp.where(mask, mine[None], 0.0).reshape(512, 128)
-        hi = part.astype(BF16)
-        lo = (part - hi.astype(F32)).astype(BF16)
-        return dot(jnp.concatenate([hi, lo], 1), jnp.concatenate([near, near], 0))
-
-    acc[...] += speed[...] * spread_face(pot_mask) + 0.25 * spread_face(trac_mask)
-    for copy in x_copies + y_copies + [z_copy] + edge_copies + face_copies:
+    both_mask = pot_mask | trac_mask
+    row256 = lax.broadcasted_iota(jnp.int32, (256, 256), 0)
+    col256 = lax.broadcasted_iota(jnp.int32, (256, 256), 1)
+    keep = ((row256 & 32) == 0) == (col256 < 128)
+    spot[...] = (keep & ((col256 & 127) == near_lane)).astype(F32).astype(BF16)
+    for copy in x_copies + y_copies + [z_copy] + part_copies + edge_copies + face_copies:
         copy.wait_send()
+    cut = len(face_copies) // 2
+    mine = part[0]
+    for first, last in ((cut, len(face_copies)), (0, cut)):
+        if first < last:
+            for k in range(last - 1, first - 1, -1):
+                face_copies[k].wait_recv()
+            mine = mine + jnp.sum(face_in[first:last].astype(F32), axis=0)
+    hi = mine.astype(BF16).astype(F32)
+    lo = mine - hi
+    hi = jnp.where(both_mask, hi[None], 0.0).reshape(512, 128).astype(BF16)
+    lo = jnp.where(both_mask, lo[None], 0.0).reshape(512, 128).astype(BF16)
+    sides = dot(jnp.concatenate([hi, lo], 1), spot[...])
+    acc[...] += speed[...] * sides[:, :128] + 0.25 * sides[:, 128:]
 
 
 def write_out(ga, ba, ga_h, ba_h, sem):
@@ -339,7 +359,7 @@
         speed.reshape(512, 128),
         jnp.asarray(tsyn), jnp.asarray(tana), jnp.asarray(grad), jnp.asarray(div),
     ]
-    n_copies = 5 + 2 + ny * nz - 1
+    n_copies = 5 + 2 + ny - 1 + nz - 1
     hbm = pl.BlockSpec(memory_space=pltpu.HBM)
     vmem = pltpu.VMEM
     scratch = [vmem(a.shape, a.dtype) for a in args] + [
@@ -360,13 +380,17 @@
         vmem((2, 32, 128), F32),
         vmem((8, 128), F32),
         vmem((8, 128), F32),
+        vmem((256, 256), BF16),
         vmem((256, 128), BF16),
         vmem((ny * nz * 8, 256), BF16),
+        vmem((ny - 1, nz, 8, 128), BF16),
+        vmem((nz, 8, 128), BF16),
         vmem((ny * nz, 8, 128), BF16),
-        vmem((ny * nz - 1, 8, 128), BF16),
+        vmem((nz - 1, 8, 128), BF16),
         pltpu.SemaphoreType.DMA((15,)),
         pltpu.SemaphoreType.DMA((n_copies,)),
         pltpu.SemaphoreType.DMA((n_copies,)),
+        pltpu.SemaphoreType.REGULAR((2,)),
     ]
     ga, ba = pl.pallas_call(
         functools.partial(kernel, ny, nz, nb),
@@ -393,7 +417,7 @@
 
 def solution(mesh):
     n_mer = mesh.shape["mer"]
-    nz = NZ_FULL if n_mer == 64 else 2
+    nz = NZ_FULL if n_mer == 64 else 4
     d = P(("mer", "grp", "box"))
     return jax.shard_map(
         functools.partial(shards, n_mer // nz, nz, mesh.shape["box"]),

time: 30.1 us -> 28.6 us (0.950)
  the two profiles are of different devices: /device:TPU:8 before, /device:TPU:6 now
where the time goes in v3:
time: 28.6 us; the launch traced here: 28.4 us
  Pallas kernels  27.8 us (97%)
  between operations  0.64 us (2%)
    pallas_call x1, Pallas kernels, shards(): pl.pallas_call(functools.partial(kernel, ny, nz, nb), out_shape=(vmem((25...  27 us
    pallas_call x1, Pallas kernels, shards(): pl.pallas_call(write_out, out_shape=(jax.ShapeDtypeStruct((25, 2, 1024),...  0.79 us

profile of v3, /device:TPU:6, one launch (start us, length us, event | category | flops | bytes accessed | tf_op | source)
XLA Modules:
  0.0 28.4 jit_solution(9706798726561908286)
XLA Ops:
  0.6 27.0 %step.1 = (f32[25,2,1024]{2,1,0:T(2,128)S(1)}, f32[512,128]{1,0:T(8,128)S(1)}) custom-call(f32[25,2,1024]{2,1,0:T(2,128)} %bitcast.21, f32[5,2,5]{2,1,0:T(2,128)} %bitcast.23, bf16[25,2,1024]{2,1,0:T(2,128)(2,1)} %bitcast.22, f32[5,2,5]{2,1,0:T(2,128)} %bitcast.24, s32[1,2]{1,0:T(1,128)} %bitcast.25, s32[1,128]{1,0:T(1,128)} %bitcast.26, s32[1,128]{1,0:T(1,128)} %bitcast.27, ...), custom_call_target="tpu_custom_call" | custom-call | tf_op jit(solution)/shard_map/step/pallas_call | solution.py:395
  27.6 0.8 %write_out.1 = (f32[25,2,1024]{2,1,0:T(2,128)}, f32[512,128]{1,0:T(8,128)}) custom-call(f32[25,2,1024]{2,1,0:T(2,128)S(1)} %get-tuple-element.6.ga, f32[512,128]{1,0:T(8,128)S(1)} %get-tuple-element.7.ba), custom_call_target="tpu_custom_call" | custom-call | tf_op jit(solution)/shard_map/write_out/pallas_call | solution.py:406

commit v4 on v3

--- a/solution.py
+++ b/solution.py
@@ -43,9 +43,7 @@
     angle = (order[:, None] * sample[None, :] % 1024) * (2.0 * math.pi / 1024)
     weight = np.where(order == 0, 1.0, 2.0)[:, None]
     synthesis = np.concatenate([weight * np.cos(angle), -weight * np.sin(angle)], 0)
-    analysis = np.concatenate([np.cos(angle), -np.sin(angle)], 0).T / 1024
     synthesis = synthesis.astype(np.float32).astype(ml_dtypes.bfloat16)
-    analysis = analysis.astype(np.float32).astype(ml_dtypes.bfloat16)
     deriv = gll_derivative()
     eye5, eye2 = np.eye(5, dtype=np.float32), np.eye(2, dtype=np.float32)
     d1 = np.zeros((RP, RP), np.float32)
@@ -59,7 +57,7 @@
     )
     h1, l1, h2, l2 = h1.T, l1.T, h2.T, l2.T
     div = np.concatenate([h1, h2, h1, h2, l1, l2], 1)
-    return synthesis[:, :512], analysis, grad, div
+    return synthesis[:, :512], grad, div
 
 
 def dot(a, b):
@@ -68,9 +66,9 @@
 
 def kernel(
     ny, nz, nb,
-    disp_h, rad_h, mod_h, imass_h, cnt_h, sp_h, ro_h, fs_h, ws_h, box_h, speed_h, tsyn_h, tana_h, grad_h, div_h,
+    disp_h, rad_h, mod_h, imass_h, cnt_h, sp_h, ro_h, fs_h, ws_h, box_h, speed_h, tsyn_h, grad_h, div_h,
     ga, acc,
-    disp, rad, mod, imass, cnt, sp, ro, fs, ws, box, speed, tsyn, tana, gradm, divm,
+    disp, rad, mod, imass, cnt, sp, ro, fs, ws, box, speed, tsyn, gradm, divm,
     field, modf, radf, massf, lhs1, lhs2, pots, tracs, gather, divs,
     edge, edge_in, xin, yout, yin, zout, zin, spot, vals, route, part_in, line, face, face_in,
     in_sem, send_sem, recv_sem, relay_sem,
@@ -113,14 +111,15 @@
     for index, (src, dst) in enumerate(
         [
             (disp_h, disp), (cnt_h, cnt), (rad_h, rad), (grad_h, gradm), (tsyn_h, tsyn), (mod_h, mod), (sp_h, sp),
-            (ws_h, ws), (ro_h, ro), (fs_h, fs), (box_h, box), (tana_h, tana), (div_h, divm), (speed_h, speed),
+            (ws_h, ws), (ro_h, ro), (fs_h, fs), (box_h, box), (div_h, divm), (speed_h, speed),
             (imass_h, imass),
         ]
     ):
         copy = pltpu.make_async_copy(src, dst, in_sem.at[index])
-        copy.start()
+        if index < 10:
+            copy.start()
         loads.append(copy)
-    (l_disp, l_cnt, l_rad, l_grad, l_tsyn, l_mod, l_sp, l_ws, l_ro, l_fs, l_box, l_tana, l_div, l_speed, l_imass) = loads
+    (l_disp, l_cnt, l_rad, l_grad, l_tsyn, l_mod, l_sp, l_ws, l_ro, l_fs, l_box, l_div, l_speed, l_imass) = loads
 
     counter = [0]
 
@@ -193,32 +192,21 @@
     for i in range(25):
         modf[2 * i : 2 * i + 2, :] = mod[i].astype(F32)
     l_tsyn.wait()
+    for copy in (l_box, l_div, l_speed, l_imass):
+        copy.start()
     for s in range(2):
         half = slice(s * 512, (s + 1) * 512)
         phys = dot(lhs1[s * 256 : (s + 1) * 256, :], tsyn[...])
         for c in range(3):
-            lhs2[c * RP : (c + 1) * RP, half] = (modf[:, half] * phys[c * RP : (c + 1) * RP]).astype(BF16)
+            lhs2[s * 192 + c * RP : s * 192 + (c + 1) * RP, :] = (modf[:, half] * phys[c * RP : (c + 1) * RP]).astype(BF16)
         for t in range(4):
             b = s * 4 + t
             pots[b * RP : (b + 1) * RP, :] = phys[192:256, t * 128 : (t + 1) * 128].astype(BF16)
 
-    l_box.wait()
-    yout[0:32, :] = box[pl.ds(0, 32, stride=16), :]
-    yout[32:64, :] = box[pl.ds(15, 32, stride=16), :]
-    far_lane = 127 * (1 - grp)
-    near_lane = 127 * grp
-    row128 = lax.broadcasted_iota(jnp.int32, (128, 128), 0)
-    pick = (row128 == far_lane).astype(F32).astype(BF16)
-    column = dot(box[...].astype(BF16), pick).reshape(64, 8, 128)
-    block64 = lax.broadcasted_iota(jnp.int32, (64, 1, 128), 0)
-    lane64 = lax.broadcasted_iota(jnp.int32, (64, 1, 128), 2)
-    place = (block64 >> 1) + (block64 & 1) * 64
-    pot_mask = lane64 == place
-    trac_mask = lane64 == place + 32
-    zout[...] = jnp.sum(jnp.where(pot_mask, column, 0.0), axis=0)
-    l_tana.wait()
-    coeffs = dot(lhs2[...], tana[...])
-    c1, c2, c3 = coeffs[0:64] * mask, coeffs[64:128] * mask, coeffs[128:192] * mask
+    coeffs = lax.dot_general(lhs2[...], tsyn[...], (((1,), (1,)), ((), ())), preferred_element_type=F32)
+    scale = mask * jnp.where(order == 0, 1.0 / 1024, 1.0 / 2048)
+    signed = scale * (1 - 2 * (order & 1)).astype(F32)
+    c1, c2, c3 = (coeffs[c * RP : (c + 1) * RP] * scale + coeffs[192 + c * RP : 256 + c * RP] * signed for c in range(3))
 
     c2hi = c2.astype(BF16)
     synth = dot(jnp.concatenate([c2hi, c2hi * sign], 0), tsyn[...]).astype(BF16)
@@ -242,6 +230,20 @@
     part_copies = [
         remote(face.at[pl.ds(step * nz, nz)], part_in.at[k], y_peers[k]) for k, step in enumerate(y_ahead)
     ]
+    l_box.wait()
+    yout[0:32, :] = box[pl.ds(0, 32, stride=16), :]
+    yout[32:64, :] = box[pl.ds(15, 32, stride=16), :]
+    far_lane = 127 * (1 - grp)
+    near_lane = 127 * grp
+    row128 = lax.broadcasted_iota(jnp.int32, (128, 128), 0)
+    pick = (row128 == far_lane).astype(F32).astype(BF16)
+    column = dot(box[...].astype(BF16), pick).reshape(64, 8, 128)
+    block64 = lax.broadcasted_iota(jnp.int32, (64, 1, 128), 0)
+    lane64 = lax.broadcasted_iota(jnp.int32, (64, 1, 128), 2)
+    place = (block64 >> 1) + (block64 & 1) * 64
+    pot_mask = lane64 == place
+    trac_mask = lane64 == place + 32
+    zout[...] = jnp.sum(jnp.where(pot_mask, column, 0.0), axis=0)
     x_copies = [
         remote(box.at[pl.ds(0, 16)], xin.at[1], mer_down),
         remote(box.at[pl.ds(496, 16)], xin.at[0], mer_up),
@@ -344,7 +346,7 @@
 
 
 def shards(ny, nz, nb, displacement, radius, bulk, imass, counts, source, owner, slot, window, box, speed):
-    tsyn, tana, grad, div = constants()
+    tsyn, grad, div = constants()
     args = [
         displacement.transpose(1, 2, 0, 3).reshape(25, 2, 1024),
         radius.transpose(1, 0, 2),
@@ -357,7 +359,7 @@
         window.reshape(1, NREC),
         box.reshape(512, 128),
         speed.reshape(512, 128),
-        jnp.asarray(tsyn), jnp.asarray(tana), jnp.asarray(grad), jnp.asarray(div),
+        jnp.asarray(tsyn), jnp.asarray(grad), jnp.asarray(div),
     ]
     n_copies = 5 + 2 + ny - 1 + nz - 1
     hbm = pl.BlockSpec(memory_space=pltpu.HBM)
@@ -368,7 +370,7 @@
         vmem((RP, 128), F32),
         vmem((RP, 128), F32),
         vmem((512, 1024), BF16),
-        vmem((192, 1024), BF16),
+        vmem((384, 512), BF16),
         vmem((512, 128), BF16),
         vmem((512, 128), BF16),
         vmem((256, 512), BF16),
@@ -387,7 +389,7 @@
         vmem((nz, 8, 128), BF16),
         vmem((ny * nz, 8, 128), BF16),
         vmem((nz - 1, 8, 128), BF16),
-        pltpu.SemaphoreType.DMA((15,)),
+        pltpu.SemaphoreType.DMA((14,)),
         pltpu.SemaphoreType.DMA((n_copies,)),
         pltpu.SemaphoreType.DMA((n_copies,)),
         pltpu.SemaphoreType.REGULAR((2,)),

time: 28.6 us -> 28.2 us (0.986)
  Pallas kernels: 27.8 us -> 27.5 us
    pallas_call x1, Pallas kernels: 27 us -> 26.7 us  [shards(): pl.pallas_call(functools.partial(kernel, ny, nz, nb), out_shape=(vmem((25...]
where the time goes in v4:
time: 28.2 us; the launch traced here: 28.1 us
  Pallas kernels  27.5 us (98%)
  between operations  0.64 us (2%)
    pallas_call x1, Pallas kernels, shards(): pl.pallas_call(functools.partial(kernel, ny, nz, nb), out_shape=(vmem((25...  26.7 us
    pallas_call x1, Pallas kernels, shards(): pl.pallas_call(write_out, out_shape=(jax.ShapeDtypeStruct((25, 2, 1024),...  0.79 us

profile of v4, /device:TPU:6, one launch (start us, length us, event | category | flops | bytes accessed | tf_op | source)
XLA Modules:
  0.0 28.1 jit_solution(16949265376478050471)
XLA Ops:
  0.6 26.7 %step.1 = (f32[25,2,1024]{2,1,0:T(2,128)S(1)}, f32[512,128]{1,0:T(8,128)S(1)}) custom-call(f32[25,2,1024]{2,1,0:T(2,128)} %bitcast.21, f32[5,2,5]{2,1,0:T(2,128)} %bitcast.23, bf16[25,2,1024]{2,1,0:T(2,128)(2,1)} %bitcast.22, f32[5,2,5]{2,1,0:T(2,128)} %bitcast.24, s32[1,2]{1,0:T(1,128)} %bitcast.25, s32[1,128]{1,0:T(1,128)} %bitcast.26, s32[1,128]{1,0:T(1,128)} %bitcast.27, ...), custom_call_target="tpu_custom_call" | custom-call | tf_op jit(solution)/shard_map/step/pallas_call | solution.py:397
  27.3 0.8 %write_out.1 = (f32[25,2,1024]{2,1,0:T(2,128)}, f32[512,128]{1,0:T(8,128)}) custom-call(f32[25,2,1024]{2,1,0:T(2,128)S(1)} %get-tuple-element.6.ga, f32[512,128]{1,0:T(8,128)S(1)} %get-tuple-element.7.ba), custom_call_target="tpu_custom_call" | custom-call | tf_op jit(solution)/shard_map/write_out/pallas_call | solution.py:408

commit v5 on v4

--- a/solution.py
+++ b/solution.py
@@ -203,10 +203,15 @@
             b = s * 4 + t
             pots[b * RP : (b + 1) * RP, :] = phys[192:256, t * 128 : (t + 1) * 128].astype(BF16)
 
-    coeffs = lax.dot_general(lhs2[...], tsyn[...], (((1,), (1,)), ((), ())), preferred_element_type=F32)
     scale = mask * jnp.where(order == 0, 1.0 / 1024, 1.0 / 2048)
     signed = scale * (1 - 2 * (order & 1)).astype(F32)
-    c1, c2, c3 = (coeffs[c * RP : (c + 1) * RP] * scale + coeffs[192 + c * RP : 256 + c * RP] * signed for c in range(3))
+
+    def analyse(c):
+        rows = jnp.concatenate([lhs2[c * RP : (c + 1) * RP, :], lhs2[192 + c * RP : 256 + c * RP, :]], 0)
+        sums = lax.dot_general(rows, tsyn[...], (((1,), (1,)), ((), ())), preferred_element_type=F32)
+        return sums[:RP] * scale + sums[RP:] * signed
+
+    c2 = analyse(1)
 
     c2hi = c2.astype(BF16)
     synth = dot(jnp.concatenate([c2hi, c2hi * sign], 0), tsyn[...]).astype(BF16)
@@ -254,6 +259,7 @@
     ]
     z_copy = remote(zout, zin, other)
 
+    c1, c3 = analyse(0), analyse(2)
     c1hi = c1.astype(BF16)
     c1lo = (c1 - c1hi.astype(F32)).astype(BF16)
     c2lo = (c2 - c2hi.astype(F32)).astype(BF16)

time: 28.2 us -> 28.1 us (level)
  no operation moved by 1% of the time
where the time goes in v5:
time: 28.1 us; the launch traced here: 28 us
  Pallas kernels  27.3 us (97%)
  between operations  0.64 us (2%)
    pallas_call x1, Pallas kernels, shards(): pl.pallas_call(functools.partial(kernel, ny, nz, nb), out_shape=(vmem((25...  26.5 us
    pallas_call x1, Pallas kernels, shards(): pl.pallas_call(write_out, out_shape=(jax.ShapeDtypeStruct((25, 2, 1024),...  0.79 us

profile of v5, /device:TPU:6, one launch (start us, length us, event | category | flops | bytes accessed | tf_op | source)
XLA Modules:
  0.0 28.0 jit_solution(887059597631058602)
XLA Ops:
  0.6 26.5 %step.1 = (f32[25,2,1024]{2,1,0:T(2,128)S(1)}, f32[512,128]{1,0:T(8,128)S(1)}) custom-call(f32[25,2,1024]{2,1,0:T(2,128)} %bitcast.21, f32[5,2,5]{2,1,0:T(2,128)} %bitcast.23, bf16[25,2,1024]{2,1,0:T(2,128)(2,1)} %bitcast.22, f32[5,2,5]{2,1,0:T(2,128)} %bitcast.24, s32[1,2]{1,0:T(1,128)} %bitcast.25, s32[1,128]{1,0:T(1,128)} %bitcast.26, s32[1,128]{1,0:T(1,128)} %bitcast.27, ...), custom_call_target="tpu_custom_call" | custom-call | tf_op jit(solution)/shard_map/step/pallas_call | solution.py:403
  27.2 0.8 %write_out.1 = (f32[25,2,1024]{2,1,0:T(2,128)}, f32[512,128]{1,0:T(8,128)}) custom-call(f32[25,2,1024]{2,1,0:T(2,128)S(1)} %get-tuple-element.6.ga, f32[512,128]{1,0:T(8,128)S(1)} %get-tuple-element.7.ba), custom_call_target="tpu_custom_call" | custom-call | tf_op jit(solution)/shard_map/write_out/pallas_call | solution.py:414

commit v6 on v4

--- a/solution.py
+++ b/solution.py
@@ -227,8 +227,13 @@
     pl.semaphore_wait(barrier, len(partners))
     pl.semaphore_signal(relay_sem.at[0], inc=1, device_id=relay_up, device_id_type=MESH)
     pl.semaphore_signal(relay_sem.at[1], inc=1, device_id=relay_down, device_id_type=MESH)
+    pieces = [(nz // 4, nz // 2), (0, nz // 4), (3 * nz // 4, nz // 4)]
     part_copies = [
-        remote(face.at[pl.ds(step * nz, nz)], part_in.at[k], y_peers[k]) for k, step in enumerate(y_ahead)
+        [
+            remote(face.at[pl.ds(step * nz + lo, n)], part_in.at[k, pl.ds(lo, n)], y_peers[k])
+            for k, step in enumerate(y_ahead)
+        ]
+        for lo, n in pieces
     ]
     l_box.wait()
     yout[0:32, :] = box[pl.ds(0, 32, stride=16), :]
@@ -281,14 +286,21 @@
     total = total + jnp.where(lane512 == 0, 0.0, pltpu.roll(b, 1, 1)) + jnp.where(lane512 == 127, 0.0, pltpu.roll(b, 127, 1))
     acc[...] = speed[...] * (total - 6.0 * b)
 
-    part = face[0:nz].astype(F32)
-    for k, copy in enumerate(part_copies):
-        copy.wait_recv()
-        part = part + part_in[k].astype(F32)
-    line[...] = part.astype(BF16)
-    pl.semaphore_wait(relay_sem.at[0], 1)
-    pl.semaphore_wait(relay_sem.at[1], 1)
-    face_copies = [remote(line.at[step], face_in.at[k], z_peers[k]) for k, step in enumerate(z_ahead)]
+    face_copies = []
+    for (lo, n), copies in zip(pieces, part_copies):
+        part = face[lo : lo + n].astype(F32)
+        for k, copy in enumerate(copies):
+            copy.wait_recv()
+            part = part + part_in[k, lo : lo + n].astype(F32)
+        line[lo : lo + n] = part.astype(BF16)
+        if lo == 0:
+            own = part[0]
+        if not face_copies:
+            pl.semaphore_wait(relay_sem.at[0], 1)
+            pl.semaphore_wait(relay_sem.at[1], 1)
+        for k, step in enumerate(z_ahead):
+            if lo <= step < lo + n:
+                face_copies.append(remote(line.at[step], face_in.at[k], z_peers[k]))
 
     for copy in x_copies + y_copies + [z_copy]:
         copy.wait_recv()
@@ -320,10 +332,10 @@
     col256 = lax.broadcasted_iota(jnp.int32, (256, 256), 1)
     keep = ((row256 & 32) == 0) == (col256 < 128)
     spot[...] = (keep & ((col256 & 127) == near_lane)).astype(F32).astype(BF16)
-    for copy in x_copies + y_copies + [z_copy] + part_copies + edge_copies + face_copies:
+    for copy in x_copies + y_copies + [z_copy] + sum(part_copies, []) + edge_copies + face_copies:
         copy.wait_send()
     cut = len(face_copies) // 2
-    mine = part[0]
+    mine = own
     for first, last in ((cut, len(face_copies)), (0, cut)):
         if first < last:
             for k in range(last - 1, first - 1, -1):
@@ -361,7 +373,7 @@
         speed.reshape(512, 128),
         jnp.asarray(tsyn), jnp.asarray(grad), jnp.asarray(div),
     ]
-    n_copies = 5 + 2 + ny - 1 + nz - 1
+    n_copies = 5 + 2 + 3 * (ny - 1) + nz - 1
     hbm = pl.BlockSpec(memory_space=pltpu.HBM)
     vmem = pltpu.VMEM
     scratch = [vmem(a.shape, a.dtype) for a in args] + [

time: 28.2 us -> 28 us (level)
  Pallas kernels: 27.5 us -> 27.2 us
where the time goes in v6:
time: 28 us; the launch traced here: 27.9 us
  Pallas kernels  27.2 us (97%)
  between operations  0.64 us (2%)
    pallas_call x1, Pallas kernels, shards(): pl.pallas_call(functools.partial(kernel, ny, nz, nb), out_shape=(vmem((25...  26.4 us
    pallas_call x1, Pallas kernels, shards(): pl.pallas_call(write_out, out_shape=(jax.ShapeDtypeStruct((25, 2, 1024),...  0.79 us

profile of v6, /device:TPU:6, one launch (start us, length us, event | category | flops | bytes accessed | tf_op | source)
XLA Modules:
  0.0 27.9 jit_solution(2684140874677280282)
XLA Ops:
  0.6 26.4 %step.1 = (f32[25,2,1024]{2,1,0:T(2,128)S(1)}, f32[512,128]{1,0:T(8,128)S(1)}) custom-call(f32[25,2,1024]{2,1,0:T(2,128)} %bitcast.21, f32[5,2,5]{2,1,0:T(2,128)} %bitcast.23, bf16[25,2,1024]{2,1,0:T(2,128)(2,1)} %bitcast.22, f32[5,2,5]{2,1,0:T(2,128)} %bitcast.24, s32[1,2]{1,0:T(1,128)} %bitcast.25, s32[1,128]{1,0:T(1,128)} %bitcast.26, s32[1,128]{1,0:T(1,128)} %bitcast.27, ...), custom_call_target="tpu_custom_call" | custom-call | tf_op jit(solution)/shard_map/step/pallas_call | solution.py:409
  27.1 0.8 %write_out.1 = (f32[25,2,1024]{2,1,0:T(2,128)}, f32[512,128]{1,0:T(8,128)}) custom-call(f32[25,2,1024]{2,1,0:T(2,128)S(1)} %get-tuple-element.6.ga, f32[512,128]{1,0:T(8,128)S(1)} %get-tuple-element.7.ba), custom_call_target="tpu_custom_call" | custom-call | tf_op jit(solution)/shard_map/write_out/pallas_call | solution.py:420
